TPU v7x, 128 devices: a whole 4x4x4 slice. The times are simulated.
128 devices in a mesh: proj: 8 (over x, core), slab: 16 (over z, y).
Axes of the slice: x: 4, y: 4, z: 4, core: 2. Of those that a mesh axis runs over, the one named last changes fastest.
Arguments:
- projections: bfloat16 [2048, 64, 2048], P(('proj', 'slab')), may hold values from -6 to 6
- intersection: int32 [2048, 2], P(('proj', 'slab')), may hold values from 0 to 15, all different within a row; in each aligned block of 16 rows (0 to 15, 16 to 31, ...) at most 4 rows name the same one
- tiles: int32 [2048, 2], P(('proj', 'slab')), may hold values from 0 to 3
- tile_gain: float32 [4, 2048], replicated, may hold values from 0.25 to 4
- bp_matrix: bfloat16 [4, 2048, 1024], replicated, may hold values from -0.0078125 to 0.0078125
- lift_kernel: float32 [32, 27], replicated, may hold values from -1.25 to 1.25
- lift_bias: float32 [32], replicated, may hold values from -3 to 3
- mix_kernel: bfloat16 [27, 32], replicated, may hold values from -0.21875 to 0.21875
Outputs:
- image: float32 [64, 16, 1024], P('slab', None, 'proj')
Inputs may be any that keep to these rules, and one draw needn't show every extreme that they name: `intersection`: each view lists 2 different slabs; among the views of one device no slab is listed more than 4 times, a bound that some block reaches.
All inputs are finite; a program needn't handle non-finite values.
Results may differ from a plain program's by a relative error of at most 0.0047.
Values may be sent and summed in bfloat16 or wider, within the bound.
A program may use at most 128 MiB of HBM per device.

v0:
```python
import math

import jax
import jax.numpy as jnp
from jax import lax
from jax.sharding import PartitionSpec as P

VZ = 4
NY = 16


def extended(cells, sides, width):
    for axis, dim in sides:
        count = lax.axis_size(axis)
        ends = count - 1
        head = lax.slice_in_dim(cells, 0, width, axis=dim)
        tail = lax.slice_in_dim(cells, cells.shape[dim] - width, cells.shape[dim], axis=dim)
        cells = jnp.concatenate(
            [
                lax.ppermute(tail, axis, [(i, (i + 1) % count) for i in range(ends)]),
                cells,
                lax.ppermute(head, axis, [((i + 1) % count, i) for i in range(ends)]),
            ],
            axis=dim,
        )
    return cells


def hilbert_kernel(size):
    places = jnp.arange(size, dtype=jnp.int32)
    lags = places[None, :] - places[:, None]
    odd = lags % 2 != 0
    safe = jnp.where(odd, lags, 1).astype(jnp.float32)
    return jnp.where(odd, 2.0 / (math.pi * safe), jnp.float32(0.0)).astype(jnp.bfloat16)


def shifted_stack(padded, depth, height, width):
    planes = []
    for shift_z in range(3):
        for shift_y in range(3):
            for shift_x in range(3):
                planes.append(
                    padded[
                        ...,
                        shift_z : shift_z + depth,
                        shift_y : shift_y + height,
                        shift_x : shift_x + width,
                    ]
                )
    return jnp.stack(planes, 0)


def tile_lookup(tile_of, tile_gain):
    tile_ids = jnp.arange(tile_gain.shape[0], dtype=jnp.int32)
    select = (tile_of[:, None] == tile_ids[None, :]).astype(jnp.float32)
    return jnp.dot(select, tile_gain, precision=lax.Precision.HIGHEST)


def shards(
    projections, intersection, tiles, tile_gain, bp_matrix, lift_kernel, lift_bias, mix_kernel
):
    nblk, drows, det = projections.shape
    top = intersection.shape[1]
    ntile = bp_matrix.shape[0]
    wide = bp_matrix.shape[2]
    n_slab = lax.axis_size("slab")
    kernel = hilbert_kernel(det)
    filtered = jnp.dot(
        projections.reshape(nblk * drows, det), kernel, preferred_element_type=jnp.float32
    )
    filtered = filtered.astype(jnp.bfloat16).reshape(nblk, drows, det)
    dest = intersection.reshape(nblk * top)
    tile_of = tiles.reshape(nblk * top)
    slab_ids = jnp.arange(n_slab, dtype=jnp.int32)
    tile_ids = jnp.arange(ntile, dtype=jnp.int32)
    capacity = max(2, 2 * nblk * top // n_slab)
    slots = n_slab * capacity
    hits = (dest[:, None] == slab_ids[None, :]).astype(jnp.int32)
    before = jnp.cumsum(hits, axis=0) - hits
    rank = jnp.sum(before * hits, axis=1)
    slot_of = dest * capacity + rank
    picked = jnp.arange(slots, dtype=jnp.int32)[:, None] == slot_of[None, :]
    pick_views = jnp.sum(picked.reshape(slots, nblk, top).astype(jnp.int32), axis=2).astype(
        jnp.bfloat16
    )
    outbound = jnp.dot(
        pick_views, filtered.reshape(nblk, drows * det), preferred_element_type=jnp.float32
    )
    outbound = outbound.astype(jnp.bfloat16).reshape(slots, drows, det)
    slot_tile = jnp.sum(jnp.where(picked, tile_of[None, :] + 1, 0), axis=1) - 1
    inbound, in_tile = (
        lax.all_to_all(outbound, "slab", split_axis=0, concat_axis=0, tiled=True),
        lax.all_to_all(slot_tile, "slab", split_axis=0, concat_axis=0, tiled=True),
    )
    gains = tile_lookup(in_tile, tile_gain)
    weighted = (inbound.astype(jnp.float32) * gains[:, None, :]).astype(jnp.bfloat16)
    grouping = (tile_ids[:, None] == in_tile[None, :]).astype(jnp.float32)
    per_tile = jnp.dot(
        grouping,
        weighted.reshape(slots, drows * det).astype(jnp.float32),
        precision=lax.Precision.HIGHEST,
    )
    per_tile = per_tile.reshape(ntile, drows, det)
    partial_value = jnp.zeros((drows, wide), jnp.float32)
    for tile in range(ntile):
        partial_value = partial_value + jnp.dot(
            per_tile[tile], bp_matrix[tile].astype(jnp.float32), precision=lax.Precision.HIGHEST
        )
    share = lax.psum_scatter(partial_value, "proj", scatter_dimension=1, tiled=True)
    xcells = share.shape[1]
    volume = share.reshape(VZ, NY, xcells)
    rim = extended(volume, (("proj", 2), ("slab", 0)), 1)
    rim = jnp.pad(rim, ((0, 0), (1, 1), (0, 0)))
    stack = shifted_stack(rim, VZ, NY, xcells)
    lifted = jnp.einsum("co,ozyx->czyx", lift_kernel, stack, precision=lax.Precision.HIGHEST)
    features = jnp.maximum(lifted + lift_bias[:, None, None, None], 0.0).astype(jnp.bfloat16)
    frame = extended(features, (("proj", 3), ("slab", 1)), 1)
    frame = jnp.pad(frame, ((0, 0), (0, 0), (1, 1), (0, 0)))
    mixed = jnp.einsum("oc,czyx->ozyx", mix_kernel, frame, preferred_element_type=jnp.float32)
    image = volume
    for shift_z in range(3):
        for shift_y in range(3):
            for shift_x in range(3):
                offset = 9 * shift_z + 3 * shift_y + shift_x
                image = (
                    image
                    + mixed[
                        offset,
                        shift_z : shift_z + VZ,
                        shift_y : shift_y + NY,
                        shift_x : shift_x + xcells,
                    ]
                )
    return image


def solution(mesh):
    placed = (
        P(("proj", "slab"), None, None),
        P(("proj", "slab"), None),
        P(("proj", "slab"), None),
        P(),
        P(),
        P(),
        P(),
        P(),
    )
    return jax.shard_map(
        shards, mesh=mesh, in_specs=placed, out_specs=P("slab", None, "proj"), check_vma=False
    )
```

profile of v0, /device:TPU:1, one launch (start us, length us, event | category | flops | bytes accessed | tf_op | source)
XLA Modules:
  0.0 480.3 jit_solution(16740412713114133239)
XLA Ops:
  6.5 0.8 copy.139
  7.3 0.1 reshape.73
  7.4 0.1 fusion.77
  7.5 0.2 select_reduce_fusion.1
  7.7 0.7 broadcast_add_fusion
  8.4 0.1 copy.140
  8.5 0.1 add.147
  8.6 0.1 select_reduce_fusion
  8.7 0.7 sub.24
  9.4 8.6 %all-to-all-start = ((s32[16,4,1]{1,2,0:T(1,128)}), s32[16,4,1]{1,2,0:T(1,128)S(1)}, u32[]{:S(2)}, u32[]{:S(2)}) async-start(s32[16,4,1]{1,2,0:T(1,128)} %bitcast), calls=%async_computation | async-start | bytes 16384 | tf_op jit(solution)/shard_map/all_to_all | solution.py:93
  18.0 0.1 reduce_sum.31
  18.1 22.4 %convert_bitcast_fusion = bf16[1024,2048]{0,1:T(8,128)(2,1)} fusion(bf16[1024,2048]{1,0:T(8,128)(2,1)} %bitcast.329), kind=kOutput, calls=%fused_computation.31 | convolution fusion | flops 8671723520 | bytes 8388608 | tf_op jit(solution)/shard_map/dot_general | solution.py:68
  40.4 6.5 %copy.143 = bf16[1024,2048]{1,0:T(8,128)(2,1)} copy(bf16[1024,2048]{0,1:T(8,128)(2,1)} %convert_bitcast_fusion) | data formatting | bytes 8388608 | tf_op jit(solution)/shard_map/convert_element_type | solution.py:71
  47.0 4.8 reshape_reshape.3
  51.8 0.1 copy.142
  51.9 0.1 convert_reduce_fusion
  51.9 12.5 %convolution_convert_fusion = bf16[64,131072]{1,0:T(8,128)(2,1)} fusion(bf16[16,131072]{1,0:T(8,128)(2,1)} %reshape_reshape.3, s32[64,16]{0,1:T(8,128)S(1)} %convert_reduce_fusion), kind=kOutput, calls=%fused_computation | convolution fusion | flops 276825088 | bytes 20975616 | tf_op jit(solution)/shard_map/dot_general | solution.py:86
  64.4 18.6 %copy.173 = bf16[8,8,64,2048]{3,2,1,0:T(8,128)(2,1)} copy(bf16[8,8,64,2048]{3,1,2,0:T(8,128)(2,1)} %bitcast.292) | data formatting | bytes 33554432
  83.0 6.7 %all-to-all-start.1 = ((bf16[64,64,2048]{2,1,0:T(8,128)(2,1)}), bf16[64,64,2048]{2,1,0:T(8,128)(2,1)}, u32[]{:S(2)}, u32[]{:S(2)}) async-start(bf16[64,64,2048]{2,1,0:T(8,128)(2,1)} %bitcast.291), calls=%async_computation.1 | async-start | bytes 33554432 | tf_op jit(solution)/shard_map/all_to_all | solution.py:92
  89.7 0.5 broadcast.91
  90.3 0.7 reduce.19
  90.9 0.1 eq.70
  91.0 0.4 fusion.74
  91.4 244.0 %all-to-all-done.1 = bf16[64,64,2048]{2,1,0:T(8,128)(2,1)} async-done(((bf16[64,64,2048]{2,1,0:T(8,128)(2,1)}), bf16[64,64,2048]{2,1,0:T(8,128)(2,1)}, u32[]{:S(2)}, u32[]{:S(2)}) %all-to-all-start.1) | async-done | bytes 16777248 | tf_op jit(solution)/shard_map/all_to_all | solution.py:92
  335.4 9.3 %multiply_convert_fusion = bf16[64,64,2048]{2,1,0:T(8,128)(2,1)S(1)} fusion(bf16[64,64,2048]{2,1,0:T(8,128)(2,1)} %all-to-all-done.1, f32[64,2048]{1,0:T(8,128)S(1)} %fusion.74), kind=kLoop, calls=%fused_computation.1 | loop fusion | flops 25165824 | bytes 34078720 | tf_op jit(solution)/shard_map/convert_element_type | solution.py:96
  344.7 24.3 %copy.174 = bf16[8,8,64,2048]{3,1,2,0:T(8,128)(2,1)S(1)} copy(bf16[8,8,64,2048]{3,2,1,0:T(8,128)(2,1)S(1)} %bitcast.293) | data formatting | bytes 33554432
  369.0 2.4 fusion.80
  371.4 5.6 %slice_reduce_fusion = (f32[131072]{0:T(1024)S(1)}, f32[131072]{0:T(1024)S(1)}, f32[131072]{0:T(1024)S(1)}, f32[131072]{0:T(1024)S(1)}) fusion(f32[4,131072]{1,0:T(4,128)S(1)} %fusion.80), kind=kLoop, calls=%fused_computation.50 | loop fusion | bytes 4194304 | tf_op jit(solution)/shard_map/slice | solution.py:107
  377.1 0.1 squeeze.109
  377.2 0.1 squeeze.107
  377.3 4.5 fusion.14
  381.8 4.5 fusion.16
  386.3 0.1 squeeze.105
  386.4 0.1 squeeze.111
  386.5 4.5 fusion.40
  391.0 5.2 %fusion.43 = f32[64,1024]{1,0:T(8,128)} fusion(f32[64,1024]{1,0:T(8,128)S(1)} %fusion.40, f32[64,2048]{1,0:T(8,128)S(1)} %squeeze.111, bf16[4,2048,1024]{2,1,0:T(8,128)(2,1)} %param.12), kind=kOutput, calls=%fused_computation.49 | convolution fusion | flops 1610678272 | bytes 5242880 | tf_op jit(solution)/shard_map/dot_general | solution.py:106
  396.2 29.3 %reduce-scatter.2.cloned.1.call-done = f32[64,128]{1,0:T(8,128)} async-done(((f32[64,1024]{1,0:T(8,128)}), f32[64,128]{1,0:T(8,128)}) %reduce-scatter.2.cloned.1.call-update) | async-done | bytes 32784 | tf_op jit(solution)/shard_map/reduce_scatter | solution.py:109
  425.5 0.9 fusion.93
  426.4 5.2 %collective-permute-start.1 = (f32[4,16,1]{2,1,0:T(8,128)S(1)}, f32[4,16,1]{2,1,0:T(8,128)S(1)}, u32[]{:S(2)}, u32[]{:S(2)}) collective-permute-start(f32[4,16,1]{2,1,0:T(8,128)S(1)} %get-tuple-element.44), channel_id=1, source_target_pairs={{16,0},{32,16},{48,32},{64,48},{80,64},{96,80},{112,96},{17,1},{33... | collective-permute-start | bytes 776 | tf_op jit(solution)/shard_map/ppermute | solution.py:22
  431.6 1.9 collective-permute-start
  433.5 1.2 collective-permute-done
  434.7 0.8 pad_maximum_fusion.8
  435.5 1.3 collective-permute-start.3
  436.8 4.2 collective-permute-start.2
  441.1 0.9 pad_maximum_fusion.4
  442.0 0.9 select_maximum_fusion
  442.9 0.2 fusion.90
  443.1 0.9 pad_maximum_fusion.3
  444.0 0.1 fusion.91
  444.1 2.1 stack.111
  446.3 1.0 fusion.36
  447.3 0.2 fusion.89
  447.6 2.8 collective-permute-start.5
  450.4 3.9 collective-permute-start.4
  454.3 4.9 %collective-permute-done.5 = bf16[32,4,16,1]{3,0,2,1:T(8,128)(2,1)S(1)} collective-permute-done((bf16[32,4,16,1]{3,0,2,1:T(8,128)(2,1)S(1)}, bf16[32,4,16,1]{3,0,2,1:T(8,128)(2,1)S(1)}, u32[]{:S(2)}, u32[]{:S(2)}) %collective-permute-start.5) | collective-permute-done | bytes 4128 | tf_op jit(solution)/shard_map/ppermute | solution.py:22
  459.2 1.2 collective-permute-done.4
  460.4 0.3 pad_maximum_fusion.2
  460.8 1.3 collective-permute-start.7
  462.1 4.6 collective-permute-start.6
  466.6 1.8 collective-permute-done.7
  468.4 1.5 collective-permute-done.6
  469.9 0.8 fusion.24
  470.8 1.8 copy.176
  472.6 0.8 fusion.47
  (22 shorter events, 0.2 us)
Async XLA Ops:
  6.5 84.5 %copy-start = (f32[4,2048]{1,0:T(4,128)S(1)}, f32[4,2048]{1,0:T(4,128)}, u32[]{:S(2)}) copy-start(f32[4,2048]{1,0:T(4,128)} %param.11) | copy-start | bytes 98308
  9.4 73.6 %all-to-all-start = ((s32[16,4,1]{1,2,0:T(1,128)}), s32[16,4,1]{1,2,0:T(1,128)S(1)}, u32[]{:S(2)}, u32[]{:S(2)}) async-start(s32[16,4,1]{1,2,0:T(1,128)} %bitcast), calls=%async_computation | async-start | bytes 16384 | tf_op jit(solution)/shard_map/all_to_all | solution.py:93
  40.4 11.4 %copy-start.3 = (s32[16,2]{0,1:T(2,128)S(1)}, s32[16,2]{0,1:T(2,128)}, u32[]{:S(2)}) copy-start(s32[16,2]{0,1:T(2,128)} %param.9) | copy-start | bytes 388
  83.0 252.4 %all-to-all-start.1 = ((bf16[64,64,2048]{2,1,0:T(8,128)(2,1)}), bf16[64,64,2048]{2,1,0:T(8,128)(2,1)}, u32[]{:S(2)}, u32[]{:S(2)}) async-start(bf16[64,64,2048]{2,1,0:T(8,128)(2,1)} %bitcast.291), calls=%async_computation.1 | async-start | bytes 33554432 | tf_op jit(solution)/shard_map/all_to_all | solution.py:92
  89.7 335.8 %reduce-scatter.2.cloned.1.call-start = ((), (), s32[]{:S(2)}) async-start(), calls=%async_computation.3 | async-start | bytes 294912 | tf_op jit(solution)/shard_map/reduce_scatter | solution.py:109
  386.4 59.9 %copy-start.2 = (f32[32,27]{1,0:T(8,128)S(1)}, f32[32,27]{1,0:T(8,128)}, u32[]{:S(2)}) copy-start(f32[32,27]{1,0:T(8,128)} %param.13) | copy-start | bytes 10372
  386.4 59.9 %copy-start.4 = (f32[32]{0:T(128)S(1)}, f32[32]{0:T(128)}, u32[]{:S(2)}) copy-start(f32[32]{0:T(128)} %param.14) | copy-start | bytes 388
  391.0 78.9 %copy-start.5 = (bf16[27,32]{1,0:T(8,128)(2,1)S(1)}, bf16[27,32]{1,0:T(8,128)(2,1)}, u32[]{:S(2)}) copy-start(bf16[27,32]{1,0:T(8,128)(2,1)} %param.15) | copy-start | bytes 5188
  426.4 7.1 %collective-permute-start.1 = (f32[4,16,1]{2,1,0:T(8,128)S(1)}, f32[4,16,1]{2,1,0:T(8,128)S(1)}, u32[]{:S(2)}, u32[]{:S(2)}) collective-permute-start(f32[4,16,1]{2,1,0:T(8,128)S(1)} %get-tuple-element.44), channel_id=1, source_target_pairs={{16,0},{32,16},{48,32},{64,48},{80,64},{96,80},{112,96},{17,1},{33... | collective-permute-start | bytes 776 | tf_op jit(solution)/shard_map/ppermute | solution.py:22
  431.6 3.1 collective-permute-start
  435.5 6.5 %collective-permute-start.3 = (f32[1,16,130]{2,1,0:T(8,128)S(1)}, f32[1,16,130]{2,1,0:T(8,128)S(1)}, u32[]{:S(2)}, u32[]{:S(2)}) collective-permute-start(f32[1,16,130]{2,1,0:T(8,128)S(1)} %get-tuple-element.34), channel_id=1, source_target_pairs={{1,0},{2,1},{3,2},{4,3},{5,4},{6,5},{7,6},{8,7},{9,8},{10,9},{11,1... | collective-permute-start | bytes 24968 | tf_op jit(solution)/shard_map/ppermute | solution.py:22
  436.8 5.2 %collective-permute-start.2 = (f32[1,16,130]{2,1,0:T(8,128)S(1)}, f32[1,16,130]{2,1,0:T(8,128)S(1)}, u32[]{:S(2)}, u32[]{:S(2)}) collective-permute-start(f32[1,16,130]{2,1,0:T(8,128)S(1)} %get-tuple-element.33), channel_id=1, source_target_pairs={{0,1},{1,2},{2,3},{3,4},{4,5},{5,6},{6,7},{7,8},{8,9},{9,10},{10,1... | collective-permute-start | bytes 24968 | tf_op jit(solution)/shard_map/ppermute | solution.py:20
  447.5 25.0 %copy-start.1 = (f32[64,128]{1,0:T(8,128)S(1)}, f32[64,128]{1,0:T(8,128)}, u32[]{:S(2)}) copy-start(f32[64,128]{1,0:T(8,128)} %reduce-scatter.2.cloned.1.call-done) | copy-start | bytes 98308
  447.6 11.7 %collective-permute-start.5 = (bf16[32,4,16,1]{3,0,2,1:T(8,128)(2,1)S(1)}, bf16[32,4,16,1]{3,0,2,1:T(8,128)(2,1)S(1)}, u32[]{:S(2)}, u32[]{:S(2)}) collective-permute-start(bf16[32,4,16,1]{3,0,2,1:T(8,128)(2,1)S(1)} %get-tuple-element.12), channel_id=1, source_target_pairs={{16,0},{32,16},{48,32},{64,48},{80,64},{96,80},{112,96},{17,1},{33... | collective-permute-start | bytes 12296 | tf_op jit(solution)/shard_map/ppermute | solution.py:22
  450.4 10.0 %collective-permute-start.4 = (bf16[32,4,16,1]{3,0,2,1:T(8,128)(2,1)S(1)}, bf16[32,4,16,1]{3,0,2,1:T(8,128)(2,1)S(1)}, u32[]{:S(2)}, u32[]{:S(2)}) collective-permute-start(bf16[32,4,16,1]{3,0,2,1:T(8,128)(2,1)S(1)} %get-tuple-element.11), channel_id=1, source_target_pairs={{0,16},{16,32},{32,48},{48,64},{64,80},{80,96},{96,112},{1,17},{17... | collective-permute-start | bytes 12296 | tf_op jit(solution)/shard_map/ppermute | solution.py:20
  460.8 7.7 %collective-permute-start.7 = (bf16[32,1,16,130]{3,0,2,1:T(8,128)(2,1)S(1)}, bf16[32,1,16,130]{3,0,2,1:T(8,128)(2,1)S(1)}, u32[]{:S(2)}, u32[]{:S(2)}) collective-permute-start(bf16[32,1,16,130]{3,0,2,1:T(8,128)(2,1)S(1)} %get-tuple-element.10), channel_id=1, source_target_pairs={{1,0},{2,1},{3,2},{4,3},{5,4},{6,5},{7,6},{8,7},{9,8},{10,9},{11,1... | collective-permute-start | bytes 399368 | tf_op jit(solution)/shard_map/ppermute | solution.py:22
  462.1 7.9 %collective-permute-start.6 = (bf16[32,1,16,130]{3,0,2,1:T(8,128)(2,1)S(1)}, bf16[32,1,16,130]{3,0,2,1:T(8,128)(2,1)S(1)}, u32[]{:S(2)}, u32[]{:S(2)}) collective-permute-start(bf16[32,1,16,130]{3,0,2,1:T(8,128)(2,1)S(1)} %get-tuple-element.9), channel_id=1, source_target_pairs={{0,1},{1,2},{2,3},{3,4},{4,5},{5,6},{6,7},{7,8},{8,9},{9,10},{10,1... | collective-permute-start | bytes 399368 | tf_op jit(solution)/shard_map/ppermute | solution.py:20
Sparse Core Ops, SparseCore 0:
  396.4 29.1 reduce-scatter.1
where the time goes:
time: 490 us; the launch traced here: 480 us
  waiting for transfers between devices  284 us (58%)
  local copies, waits for them, and re-layouts  68 us (14%)
  matrix products  58.2 us (12%)
  starting transfers between devices  40.6 us (8%)
  other arithmetic  15.9 us (3%)
  between operations  13.8 us (3%)
    all_to_all x1, waiting for transfers between devices, shards(): lax.all_to_all(outbound, 'slab', split_axis=0, concat_axis=0, tiled=True)  244 us
    unnamed x15, local copies, waits for them, and re-layouts  43.6 us
    reduce_scatter x1, waiting for transfers between devices, shards(): lax.psum_scatter(partial_value, 'proj', scatter_dimension=1, tiled=True)  29.3 us
    dot_general x1, matrix products, shards(): jnp.dot(projections.reshape(nblk * drows, det), kernel, preferred_element...  22.4 us
    dot_general x4, matrix products, shards(): jnp.dot(per_tile[tile], bp_matrix[tile].astype(jnp.float32), precision=la...  18.7 us
    ppermute x4, starting transfers between devices, extended(): lax.ppermute(tail, axis, [(i, (i + 1) % count) for i in range(ends)])  14.6 us
    dot_general x1, matrix products, shards(): jnp.dot(pick_views, filtered.reshape(nblk, drows * det), preferred_elemen...  12.5 us
    ppermute x4, starting transfers between devices, extended(): lax.ppermute(head, axis, [((i + 1) % count, i) for i in range(ends)])  10.6 us
  transfers between devices with their start and end apart: 11, of which 7 were waited for; matrix products, arithmetic and copies ran while one was open for 14% of the time, Pallas kernels for 0%

commit v1 on v0

v1 whole, which is shorter than its diff:
```python
import functools
import math

import jax
import jax.numpy as jnp
import ml_dtypes
import numpy as np
from jax import lax
from jax.experimental import pallas as pl
from jax.experimental.pallas import tpu as pltpu
from jax.sharding import PartitionSpec as P

VZ = 4
NY = 16
NB = 11
SLOTS = 4 * NB
WID = 256


def lag_strip(det):
    lag = (det - WID) + np.arange(WID)[None, :] - np.arange(2 * det - WID)[:, None]
    odd = lag % 2 != 0
    safe = np.where(odd, lag, 1).astype(np.float32)
    values = np.where(odd, np.float32(2.0) / (np.float32(math.pi) * safe), np.float32(0.0))
    return values.astype(ml_dtypes.bfloat16)


def route(inter, tiles):
    def column(a):
        nv = a.shape[0]
        return jnp.concatenate(
            [jnp.broadcast_to(a[:, k : k + 1], (nv, 128)) for k in range(2)], axis=0
        )

    tb, sb = column(tiles), column(inter)
    n = tb.shape[0]
    row = lax.broadcasted_iota(jnp.int32, (n, 128), 0)
    lane = lax.broadcasted_iota(jnp.int32, (n, 128), 1)
    lane1 = lane[0:1]

    def rank(col):
        across = jnp.sum(jnp.where(row == lane, col, 0), axis=0, keepdims=True)
        same = jnp.where((col == across) & (lane < row), 1, 0)
        return jnp.sum(same, axis=1, keepdims=True)

    ends = []
    total = jnp.zeros((1, 128), jnp.int32)
    for t in range(3):
        count = jnp.sum(jnp.where(tb == t, 1, 0), axis=0, keepdims=True)
        total = total + ((count + 3) >> 2)
        ends.append(total)
    base = jnp.where(tb == 0, 0, jnp.where(tb == 1, ends[0], jnp.where(tb == 2, ends[1], ends[2])))
    slot = 4 * base + rank(tb)
    view_row = jnp.sum(jnp.where(slot == lane, row & 15, 0), axis=0, keepdims=True)
    tile_row = sum(jnp.where(lane1 >= e, 1, 0) for e in ends)
    order = rank(sb)
    picks = [
        jnp.sum(jnp.where((sb == lane) & (order == r), slot - SLOTS, 0), axis=0, keepdims=True) + SLOTS
        for r in range(4)
    ]
    return jnp.concatenate([view_row, tile_row, view_row, tile_row] + picks, axis=0)


def kernel(
    proj_ref, strip_ref, gain_ref, inter_ref, tiles_ref, bp_ref, out_ref,
    pv, ks, bpv, fv, wv, rv, planv, plan, sems,
):
    rows, det = pv.shape
    loads = [
        pltpu.make_async_copy(proj_ref, pv, sems.at[0]),
        pltpu.make_async_copy(strip_ref, ks, sems.at[1]),
        pltpu.make_async_copy(bp_ref, bpv, sems.at[2]),
    ]
    for c in loads:
        c.start()
    planv[...] = route(inter_ref[...], tiles_ref[...])
    to_smem = pltpu.make_async_copy(planv, plan, sems.at[3])
    to_smem.start()
    rv[SLOTS * 64 :, :] = jnp.zeros((64, WID), jnp.float32)
    to_smem.wait()
    loads[0].wait()
    loads[1].wait()

    @pl.loop(0, det // WID)
    def _(b):
        k = ks[pl.ds(pl.multiple_of((det - WID) - b * WID, WID), det), :]
        acc = jnp.dot(pv[...], k, preferred_element_type=jnp.float32)
        fv[:, pl.ds(pl.multiple_of(b * WID, WID), WID)] = acc.astype(jnp.bfloat16)

    @pl.loop(0, SLOTS)
    def _(q):
        v = plan[0, q]
        t = plan[1, q // 4]
        f = fv[pl.ds(pl.multiple_of(v * 64, 64), 64), :].astype(jnp.float32)
        g = gain_ref[pl.ds(t, 1), :]
        wv[pl.ds(pl.multiple_of(q * 64, 64), 64), :] = (f * g).astype(jnp.bfloat16)

    loads[2].wait()

    for j in range(4):
        @pl.loop(0, NB)
        def _(b):
            t = plan[1, b]
            at = pl.multiple_of(b * WID, WID)
            rv[pl.ds(at, WID), :] = jnp.dot(
                wv[pl.ds(at, WID), :],
                bpv[t, :, j * WID : (j + 1) * WID],
                preferred_element_type=jnp.float32,
            )

        @pl.loop(0, 16)
        def _(s):
            total = None
            for r in range(4):
                q = plan[4 + r, s]
                term = rv[pl.ds(pl.multiple_of(q * 64, 64), 64), :]
                total = term if total is None else total + term
            out_ref[2 * j, s] = total[:, :128]
            out_ref[2 * j + 1, s] = total[:, 128:]


def backproject(projections, intersection, tiles, tile_gain, bp_matrix):
    nblk, drows, det = projections.shape
    rows = nblk * drows
    any_spec = pl.BlockSpec(memory_space=pl.ANY)
    vmem = pl.BlockSpec(memory_space=pltpu.VMEM)
    return pl.pallas_call(
        kernel,
        out_shape=jax.ShapeDtypeStruct((8, 16, drows, 128), jnp.float32),
        in_specs=[any_spec, any_spec, vmem, vmem, vmem, any_spec],
        out_specs=vmem,
        scratch_shapes=[
            pltpu.VMEM((rows, det), jnp.bfloat16),
            pltpu.VMEM((2 * det - WID, WID), jnp.bfloat16),
            pltpu.VMEM(bp_matrix.shape, jnp.bfloat16),
            pltpu.VMEM((rows, det), jnp.bfloat16),
            pltpu.VMEM((SLOTS * drows, det), jnp.bfloat16),
            pltpu.VMEM((SLOTS * drows + drows, WID), jnp.float32),
            pltpu.VMEM((8, 128), jnp.int32),
            pltpu.SMEM((8, 128), jnp.int32),
            pltpu.SemaphoreType.DMA((4,)),
        ],
        compiler_params=pltpu.CompilerParams(vmem_limit_bytes=60 * 1024 * 1024),
    )(
        projections.reshape(rows, det), jnp.asarray(lag_strip(det)), tile_gain, intersection, tiles, bp_matrix
    )


def extended(cells, sides, width):
    for axis, dim in sides:
        count = lax.axis_size(axis)
        ends = count - 1
        head = lax.slice_in_dim(cells, 0, width, axis=dim)
        tail = lax.slice_in_dim(cells, cells.shape[dim] - width, cells.shape[dim], axis=dim)
        cells = jnp.concatenate(
            [
                lax.ppermute(tail, axis, [(i, (i + 1) % count) for i in range(ends)]),
                cells,
                lax.ppermute(head, axis, [((i + 1) % count, i) for i in range(ends)]),
            ],
            axis=dim,
        )
    return cells


def shifted_stack(padded, depth, height, width):
    planes = []
    for shift_z in range(3):
        for shift_y in range(3):
            for shift_x in range(3):
                planes.append(
                    padded[
                        ...,
                        shift_z : shift_z + depth,
                        shift_y : shift_y + height,
                        shift_x : shift_x + width,
                    ]
                )
    return jnp.stack(planes, 0)


def shards(
    projections, intersection, tiles, tile_gain, bp_matrix, lift_kernel, lift_bias, mix_kernel
):
    partial = backproject(projections, intersection, tiles, tile_gain, bp_matrix)
    part = lax.psum_scatter(partial, "proj", scatter_dimension=0, tiled=False)
    share = lax.psum_scatter(part, "slab", scatter_dimension=0, tiled=False)
    xcells = share.shape[1]
    volume = share.reshape(VZ, NY, xcells)
    rim = extended(volume, (("proj", 2), ("slab", 0)), 1)
    rim = jnp.pad(rim, ((0, 0), (1, 1), (0, 0)))
    stack = shifted_stack(rim, VZ, NY, xcells)
    lifted = jnp.einsum("co,ozyx->czyx", lift_kernel, stack, precision=lax.Precision.HIGHEST)
    features = jnp.maximum(lifted + lift_bias[:, None, None, None], 0.0).astype(jnp.bfloat16)
    frame = extended(features, (("proj", 3), ("slab", 1)), 1)
    frame = jnp.pad(frame, ((0, 0), (0, 0), (1, 1), (0, 0)))
    mixed = jnp.einsum("oc,czyx->ozyx", mix_kernel, frame, preferred_element_type=jnp.float32)
    image = volume
    for shift_z in range(3):
        for shift_y in range(3):
            for shift_x in range(3):
                offset = 9 * shift_z + 3 * shift_y + shift_x
                image = (
                    image
                    + mixed[
                        offset,
                        shift_z : shift_z + VZ,
                        shift_y : shift_y + NY,
                        shift_x : shift_x + xcells,
                    ]
                )
    return image


def solution(mesh):
    placed = (
        P(("proj", "slab"), None, None),
        P(("proj", "slab"), None),
        P(("proj", "slab"), None),
        P(),
        P(),
        P(),
        P(),
        P(),
    )
    return jax.shard_map(
        shards, mesh=mesh, in_specs=placed, out_specs=P("slab", None, "proj"), check_vma=False
    )
```

time: 490 us -> 227 us (0.46)
  the two profiles are of different devices: /device:TPU:1 before, /device:TPU:29 now
where the time goes in v1:
time: 227 us
  waiting for transfers between devices  136 us (60%)
  Pallas kernels  39.3 us (17%)
  starting transfers between devices  23 us (10%)
  between operations  13.6 us (6%)
  local copies, waits for them, and re-layouts  8.04 us (4%)
  other arithmetic  4.7 us (2%)
    unnamed x3, waiting for transfers between devices  75.9 us
    pallas_call x1, Pallas kernels, backproject(): pl.pallas_call(kernel, out_shape=jax.ShapeDtypeStruct((8, 16, drows, 128)...  39.3 us
    reduce_scatter x1, waiting for transfers between devices, shards(): part = lax.psum_scatter(partial, 'proj', scatter_dimension=0, tiled=False)  36.2 us
    ppermute x4, waiting for transfers between devices, extended(): lax.ppermute(head, axis, [((i + 1) % count, i) for i in range(ends)])  15.3 us
    ppermute x4, starting transfers between devices, extended(): lax.ppermute(tail, axis, [(i, (i + 1) % count) for i in range(ends)])  13.5 us
    ppermute x4, starting transfers between devices, extended(): lax.ppermute(head, axis, [((i + 1) % count, i) for i in range(ends)])  9.4 us
    ppermute x4, waiting for transfers between devices, extended(): lax.ppermute(tail, axis, [(i, (i + 1) % count) for i in range(ends)])  8.76 us
  transfers between devices with their start and end apart: 10, of which 8 were waited for; matrix products, arithmetic and copies ran while one was open for 0% of the time, Pallas kernels for 0%

profile of v1, /device:TPU:29, one launch (start us, length us, event | category | flops | bytes accessed | tf_op | source)
XLA Modules:
  0.0 226.6 jit_solution(4372758611841722474)
XLA Ops:
  6.5 0.0 copy-start
  6.5 0.0 reduce-scatter.5.cloned.1.call-start
  6.5 1.4 copy.39.inter_ref
  7.9 1.3 copy.40.tiles_ref
  9.3 39.3 %shard_map.91 = f32[8,16,64,128]{3,2,1,0:T(8,128)} custom-call(bf16[1024,2048]{1,0:T(8,128)(2,1)} %bitcast.258, bf16[3840,256]{1,0:T(8,128)(2,1)} %constant.8.clone.strip_ref, f32[4,2048]{1,0:T(4,128)} %gain_ref.1, s32[16,2]{1,0:T(8,128)} %copy.39.inter_ref, s32[16,2]{1,0:T(8,128)} %copy.40.tiles_ref, bf16[4,2048,1024]{2,1,0:T(8,128)(2,1)} %bp_ref.1), custom_call_target="tpu_custom_call" | custom-call | tf_op jit(solution)/shard_map/pallas_call | solution.py:127
  48.6 0.0 reduce-scatter.5.cloned.1.call-update
  48.6 0.0 copy-start.2
  48.6 0.0 reduce-scatter.7.cloned.1.call-start
  48.7 36.2 %reduce-scatter.5.cloned.1.call-done = f32[1,16,64,128]{3,2,1,0:T(8,128)} async-done(((f32[8,16,64,128]{3,2,1,0:T(8,128)}), f32[1,16,64,128]{3,2,1,0:T(8,128)}) %reduce-scatter.5.cloned.1.call-update) | async-done | bytes 524304 | tf_op jit(solution)/shard_map/reduce_scatter | solution.py:186
  84.8 0.0 reduce-scatter.7.cloned.1.call-update
  84.9 75.8 %reduce-scatter.7.cloned.1.call-done = f32[1,64,128]{2,1,0:T(8,128)} async-done(((f32[16,64,128]{2,1,0:T(8,128)}), f32[1,64,128]{2,1,0:T(8,128)}) %reduce-scatter.7.cloned.1.call-update) | async-done | bytes 32784
  160.7 0.9 fusion.48
  161.6 5.6 %collective-permute-start = (f32[4,16,1]{2,1,0:T(8,128)S(1)}, f32[4,16,1]{2,1,0:T(8,128)S(1)}, u32[]{:S(2)}, u32[]{:S(2)}) collective-permute-start(f32[4,16,1]{2,1,0:T(8,128)S(1)} %get-tuple-element.39), channel_id=1, source_target_pairs={{0,16},{16,32},{32,48},{48,64},{64,80},{80,96},{96,112},{1,17},{17... | collective-permute-start | bytes 776 | tf_op jit(solution)/shard_map/ppermute | solution.py:157
  167.2 1.9 collective-permute-start.1
  169.1 0.0 collective-permute-done
  169.1 3.3 %collective-permute-done.1 = f32[4,16,1]{2,1,0:T(8,128)S(1)} collective-permute-done((f32[4,16,1]{2,1,0:T(8,128)S(1)}, f32[4,16,1]{2,1,0:T(8,128)S(1)}, u32[]{:S(2)}, u32[]{:S(2)}) %collective-permute-start.1) | collective-permute-done | bytes 288 | tf_op jit(solution)/shard_map/ppermute | solution.py:159
  172.4 0.8 pad_maximum_fusion.8
  173.2 3.1 %collective-permute-start.2 = (f32[1,16,130]{2,1,0:T(8,128)S(1)}, f32[1,16,130]{2,1,0:T(8,128)S(1)}, u32[]{:S(2)}, u32[]{:S(2)}) collective-permute-start(f32[1,16,130]{2,1,0:T(8,128)S(1)} %get-tuple-element.29), channel_id=1, source_target_pairs={{0,1},{1,2},{2,3},{3,4},{4,5},{5,6},{6,7},{7,8},{8,9},{9,10},{10,1... | collective-permute-start | bytes 24968 | tf_op jit(solution)/shard_map/ppermute | solution.py:157
  176.3 2.2 collective-permute-start.3
  178.5 0.9 pad_maximum_fusion.4
  179.5 0.0 collective-permute-done.2
  179.5 3.8 %collective-permute-done.3 = f32[1,16,130]{2,1,0:T(8,128)S(1)} collective-permute-done((f32[1,16,130]{2,1,0:T(8,128)S(1)}, f32[1,16,130]{2,1,0:T(8,128)S(1)}, u32[]{:S(2)}, u32[]{:S(2)}) %collective-permute-start.3) | collective-permute-done | bytes 8352 | tf_op jit(solution)/shard_map/ppermute | solution.py:159
  183.3 0.9 select_maximum_fusion
  184.2 0.2 fusion.45
  184.4 0.9 pad_maximum_fusion.3
  185.3 0.1 fusion.46
  185.4 2.1 stack.111
  187.5 0.0 copy-done
  187.6 0.0 copy-done.2
  187.6 0.0 copy-start.3
  187.6 1.0 fusion.12
  188.6 0.2 fusion.44
  188.9 2.9 %collective-permute-start.4 = (bf16[32,4,16,1]{3,0,2,1:T(8,128)(2,1)S(1)}, bf16[32,4,16,1]{3,0,2,1:T(8,128)(2,1)S(1)}, u32[]{:S(2)}, u32[]{:S(2)}) collective-permute-start(bf16[32,4,16,1]{3,0,2,1:T(8,128)(2,1)S(1)} %get-tuple-element.7), channel_id=1, source_target_pairs={{0,16},{16,32},{32,48},{48,64},{64,80},{80,96},{96,112},{1,17},{17... | collective-permute-start | bytes 12296 | tf_op jit(solution)/shard_map/ppermute | solution.py:157
  191.8 1.9 collective-permute-start.5
  193.7 4.2 %collective-permute-done.4 = bf16[32,4,16,1]{3,0,2,1:T(8,128)(2,1)S(1)} collective-permute-done((bf16[32,4,16,1]{3,0,2,1:T(8,128)(2,1)S(1)}, bf16[32,4,16,1]{3,0,2,1:T(8,128)(2,1)S(1)}, u32[]{:S(2)}, u32[]{:S(2)}) %collective-permute-start.4) | collective-permute-done | bytes 4128 | tf_op jit(solution)/shard_map/ppermute | solution.py:157
  197.9 4.4 %collective-permute-done.5 = bf16[32,4,16,1]{3,0,2,1:T(8,128)(2,1)S(1)} collective-permute-done((bf16[32,4,16,1]{3,0,2,1:T(8,128)(2,1)S(1)}, bf16[32,4,16,1]{3,0,2,1:T(8,128)(2,1)S(1)}, u32[]{:S(2)}, u32[]{:S(2)}) %collective-permute-start.5) | collective-permute-done | bytes 4128 | tf_op jit(solution)/shard_map/ppermute | solution.py:159
  202.3 0.3 pad_maximum_fusion.2
  202.6 1.9 collective-permute-start.6
  204.6 3.4 %collective-permute-start.7 = (bf16[32,1,16,130]{3,0,2,1:T(8,128)(2,1)S(1)}, bf16[32,1,16,130]{3,0,2,1:T(8,128)(2,1)S(1)}, u32[]{:S(2)}, u32[]{:S(2)}) collective-permute-start(bf16[32,1,16,130]{3,0,2,1:T(8,128)(2,1)S(1)} %get-tuple-element.6), channel_id=1, source_target_pairs={{1,0},{2,1},{3,2},{4,3},{5,4},{6,5},{7,6},{8,7},{9,8},{10,9},{11,1... | collective-permute-start | bytes 399368 | tf_op jit(solution)/shard_map/ppermute | solution.py:159
  207.9 4.6 %collective-permute-done.6 = bf16[32,1,16,130]{3,0,2,1:T(8,128)(2,1)S(1)} collective-permute-done((bf16[32,1,16,130]{3,0,2,1:T(8,128)(2,1)S(1)}, bf16[32,1,16,130]{3,0,2,1:T(8,128)(2,1)S(1)}, u32[]{:S(2)}, u32[]{:S(2)}) %collective-permute-start.6) | collective-permute-done | bytes 133152 | tf_op jit(solution)/shard_map/ppermute | solution.py:157
  212.5 3.7 %collective-permute-done.7 = bf16[32,1,16,130]{3,0,2,1:T(8,128)(2,1)S(1)} collective-permute-done((bf16[32,1,16,130]{3,0,2,1:T(8,128)(2,1)S(1)}, bf16[32,1,16,130]{3,0,2,1:T(8,128)(2,1)S(1)}, u32[]{:S(2)}, u32[]{:S(2)}) %collective-permute-start.7) | collective-permute-done | bytes 133152 | tf_op jit(solution)/shard_map/ppermute | solution.py:159
  216.3 0.0 copy-done.3
  216.3 0.8 fusion
  217.1 0.0 copy-start.1
  217.1 1.8 copy.70
  218.9 0.0 copy-done.1
  218.9 0.8 fusion.14
Async XLA Ops:
  6.5 181.0 %copy-start = (f32[32,27]{1,0:T(8,128)S(1)}, f32[32,27]{1,0:T(8,128)}, u32[]{:S(2)}) copy-start(f32[32,27]{1,0:T(8,128)} %param.14) | copy-start | bytes 10372
  6.5 78.3 %reduce-scatter.5.cloned.1.call-start = ((), (), s32[]{:S(2)}) async-start(), calls=%async_computation.2 | async-start | bytes 4718592 | tf_op jit(solution)/shard_map/reduce_scatter | solution.py:186
  48.6 138.9 %copy-start.2 = (f32[32]{0:T(128)S(1)}, f32[32]{0:T(128)}, u32[]{:S(2)}) copy-start(f32[32]{0:T(128)} %param.15) | copy-start | bytes 388
  48.6 112.1 %reduce-scatter.7.cloned.1.call-start = ((), (), s32[]{:S(2)}) async-start(), calls=%async_computation.3 | async-start | bytes 557056
  161.6 7.5 %collective-permute-start = (f32[4,16,1]{2,1,0:T(8,128)S(1)}, f32[4,16,1]{2,1,0:T(8,128)S(1)}, u32[]{:S(2)}, u32[]{:S(2)}) collective-permute-start(f32[4,16,1]{2,1,0:T(8,128)S(1)} %get-tuple-element.39), channel_id=1, source_target_pairs={{0,16},{16,32},{32,48},{48,64},{64,80},{80,96},{96,112},{1,17},{17... | collective-permute-start | bytes 776 | tf_op jit(solution)/shard_map/ppermute | solution.py:157
  167.2 5.2 %collective-permute-start.1 = (f32[4,16,1]{2,1,0:T(8,128)S(1)}, f32[4,16,1]{2,1,0:T(8,128)S(1)}, u32[]{:S(2)}, u32[]{:S(2)}) collective-permute-start(f32[4,16,1]{2,1,0:T(8,128)S(1)} %get-tuple-element.40), channel_id=1, source_target_pairs={{16,0},{32,16},{48,32},{64,48},{80,64},{96,80},{112,96},{17,1},{33... | collective-permute-start | bytes 776 | tf_op jit(solution)/shard_map/ppermute | solution.py:159
  173.2 6.2 %collective-permute-start.2 = (f32[1,16,130]{2,1,0:T(8,128)S(1)}, f32[1,16,130]{2,1,0:T(8,128)S(1)}, u32[]{:S(2)}, u32[]{:S(2)}) collective-permute-start(f32[1,16,130]{2,1,0:T(8,128)S(1)} %get-tuple-element.29), channel_id=1, source_target_pairs={{0,1},{1,2},{2,3},{3,4},{4,5},{5,6},{6,7},{7,8},{8,9},{9,10},{10,1... | collective-permute-start | bytes 24968 | tf_op jit(solution)/shard_map/ppermute | solution.py:157
  176.3 7.0 %collective-permute-start.3 = (f32[1,16,130]{2,1,0:T(8,128)S(1)}, f32[1,16,130]{2,1,0:T(8,128)S(1)}, u32[]{:S(2)}, u32[]{:S(2)}) collective-permute-start(f32[1,16,130]{2,1,0:T(8,128)S(1)} %get-tuple-element.30), channel_id=1, source_target_pairs={{1,0},{2,1},{3,2},{4,3},{5,4},{6,5},{7,6},{8,7},{9,8},{10,9},{11,1... | collective-permute-start | bytes 24968 | tf_op jit(solution)/shard_map/ppermute | solution.py:159
  187.6 28.7 %copy-start.3 = (bf16[27,32]{1,0:T(8,128)(2,1)S(1)}, bf16[27,32]{1,0:T(8,128)(2,1)}, u32[]{:S(2)}) copy-start(bf16[27,32]{1,0:T(8,128)(2,1)} %param.16) | copy-start | bytes 5188
  188.9 9.1 %collective-permute-start.4 = (bf16[32,4,16,1]{3,0,2,1:T(8,128)(2,1)S(1)}, bf16[32,4,16,1]{3,0,2,1:T(8,128)(2,1)S(1)}, u32[]{:S(2)}, u32[]{:S(2)}) collective-permute-start(bf16[32,4,16,1]{3,0,2,1:T(8,128)(2,1)S(1)} %get-tuple-element.7), channel_id=1, source_target_pairs={{0,16},{16,32},{32,48},{48,64},{64,80},{80,96},{96,112},{1,17},{17... | collective-permute-start | bytes 12296 | tf_op jit(solution)/shard_map/ppermute | solution.py:157
  191.8 10.5 %collective-permute-start.5 = (bf16[32,4,16,1]{3,0,2,1:T(8,128)(2,1)S(1)}, bf16[32,4,16,1]{3,0,2,1:T(8,128)(2,1)S(1)}, u32[]{:S(2)}, u32[]{:S(2)}) collective-permute-start(bf16[32,4,16,1]{3,0,2,1:T(8,128)(2,1)S(1)} %get-tuple-element.8), channel_id=1, source_target_pairs={{16,0},{32,16},{48,32},{64,48},{80,64},{96,80},{112,96},{17,1},{33... | collective-permute-start | bytes 12296 | tf_op jit(solution)/shard_map/ppermute | solution.py:159
  202.6 9.9 %collective-permute-start.6 = (bf16[32,1,16,130]{3,0,2,1:T(8,128)(2,1)S(1)}, bf16[32,1,16,130]{3,0,2,1:T(8,128)(2,1)S(1)}, u32[]{:S(2)}, u32[]{:S(2)}) collective-permute-start(bf16[32,1,16,130]{3,0,2,1:T(8,128)(2,1)S(1)} %get-tuple-element.5), channel_id=1, source_target_pairs={{0,1},{1,2},{2,3},{3,4},{4,5},{5,6},{6,7},{7,8},{8,9},{9,10},{10,1... | collective-permute-start | bytes 399368 | tf_op jit(solution)/shard_map/ppermute | solution.py:157
  204.6 11.7 %collective-permute-start.7 = (bf16[32,1,16,130]{3,0,2,1:T(8,128)(2,1)S(1)}, bf16[32,1,16,130]{3,0,2,1:T(8,128)(2,1)S(1)}, u32[]{:S(2)}, u32[]{:S(2)}) collective-permute-start(bf16[32,1,16,130]{3,0,2,1:T(8,128)(2,1)S(1)} %get-tuple-element.6), channel_id=1, source_target_pairs={{1,0},{2,1},{3,2},{4,3},{5,4},{6,5},{7,6},{8,7},{9,8},{10,9},{11,1... | collective-permute-start | bytes 399368 | tf_op jit(solution)/shard_map/ppermute | solution.py:159
  217.1 1.8 copy-start.1
Sparse Core Ops, SparseCore 0:
  48.7 36.0 reduce-scatter.4
  88.0 72.6 reduce-scatter.6

commit v2 on v1

v2 whole, which is shorter than its diff:
```python
import functools
import math

import jax
import jax.numpy as jnp
import ml_dtypes
import numpy as np
from jax import lax
from jax.experimental import pallas as pl
from jax.experimental.pallas import tpu as pltpu
from jax.sharding import PartitionSpec as P

MESH = pl.DeviceIdType.MESH
F32, BF16 = jnp.float32, jnp.bfloat16
VZ = 4
NY = 16
CH = 32
NB = 11
SLOTS = 4 * NB
WID = 256
TURN = (2, 1, 3, 0)


def lag_strip(det):
    lag = (det - WID) + np.arange(WID)[None, :] - np.arange(2 * det - WID)[:, None]
    odd = lag % 2 != 0
    safe = np.where(odd, lag, 1).astype(np.float32)
    values = np.where(odd, np.float32(2.0) / (np.float32(math.pi) * safe), np.float32(0.0))
    return values.astype(ml_dtypes.bfloat16)


def iota(shape, dim):
    return lax.broadcasted_iota(jnp.int32, shape, dim)


def route(inter, tiles):
    nv = inter.shape[1]

    def column(a):
        eye = iota((nv, nv), 0) == iota((nv, nv), 1)
        parts = [
            jnp.sum(jnp.where(eye, a[k : k + 1, :], 0), axis=1, keepdims=True) for k in range(2)
        ]
        return jnp.broadcast_to(jnp.concatenate(parts, axis=0), (2 * nv, 128))

    tb, sb = column(tiles), column(inter)
    row, lane = iota((2 * nv, 128), 0), iota((2 * nv, 128), 1)
    lane1 = lane[0:1]

    def rank(col):
        across = jnp.sum(jnp.where(row == lane, col, 0), axis=0, keepdims=True)
        same = jnp.where((col == across) & (lane < row), 1, 0)
        return jnp.sum(same, axis=1, keepdims=True)

    ends = []
    total = jnp.zeros((1, 128), jnp.int32)
    for t in range(3):
        count = jnp.sum(jnp.where(tb == t, 1, 0), axis=0, keepdims=True)
        total = total + ((count + 3) >> 2)
        ends.append(total)
    base = jnp.where(tb == 0, 0, jnp.where(tb == 1, ends[0], jnp.where(tb == 2, ends[1], ends[2])))
    slot = 4 * base + rank(tb)
    view_row = jnp.sum(jnp.where(slot == lane, row & (nv - 1), 0), axis=0, keepdims=True)
    tile_row = sum(jnp.where(lane1 >= e, 1, 0) for e in ends)
    order = rank(sb)
    picks = [
        jnp.sum(jnp.where((sb == lane) & (order == r), slot - SLOTS, 0), axis=0, keepdims=True) + SLOTS
        for r in range(4)
    ]
    return jnp.concatenate([view_row, tile_row, view_row, tile_row] + picks, axis=0)


def mm(a, b):
    return jnp.dot(a, b, preferred_element_type=F32)


def hot(mask):
    return jnp.where(mask, 1.0, 0.0).astype(BF16)


def lift_matrix(lift, bias):
    rows, cols = NY * CH, 160
    spread = hot((iota((rows, CH), 0) & (CH - 1)) == iota((rows, CH), 1))
    taps = mm(spread, lift.astype(BF16)).astype(BF16)
    o, m = iota((27, cols), 0), iota((27, cols), 1)
    dx, dz = m // 48, (m // 16) % 3
    step = (iota((rows, cols), 1) & (NY - 1)) - iota((rows, cols), 0) // CH + 1
    out = jnp.zeros((rows, cols), F32)
    for dy in range(3):
        pick = hot((o == 9 * dz + 3 * dy + dx) & (m < 144))
        out = out + jnp.where(step == dy, mm(taps, pick), 0.0)
    eye = iota((CH, CH), 0) == iota((CH, CH), 1)
    left = jnp.sum(jnp.where(eye, bias, 0.0), axis=1, keepdims=True)
    lane = iota((CH, cols), 1)
    table = jnp.zeros((CH, cols), F32)
    for k in range(3):
        head = left.astype(BF16).astype(F32)
        table = table + jnp.where(lane == 144 + k, head, 0.0)
        left = left - head
    return (out + mm(spread, table.astype(BF16))).astype(BF16)


def mix_matrix(mix):
    rows, cols = 144, NY * CH
    spread = hot((iota((CH, cols), 1) & (CH - 1)) == iota((CH, cols), 0))
    taps = mm(mix, spread).astype(BF16)
    m, o = iota((rows, 27), 0), iota((rows, 27), 1)
    dz, dx = m // 48, (m // 16) % 3
    step = iota((rows, cols), 1) // CH - (iota((rows, cols), 0) & (NY - 1)) + 1
    out = jnp.zeros((rows, cols), F32)
    for dy in range(3):
        pick = hot(o == 9 * dz + 3 * dy + dx)
        out = out + jnp.where(step == dy, mm(pick, taps), 0.0)
    return out.astype(BF16)


def kernel(
    proj_ref, strip_ref, gain_ref, inter_ref, tiles_ref, bp_ref, lift_ref, bias_ref, mix_ref, out_ref,
    pv, ks, bp0, bp1, bp2, bp3, fa, fb, gainv, wv, rv, own, psend, prec, xsend, xrec, ysend, yrec, vol, hsend, hrec, wlift, wmix,
    planv, plan, lsem, ps, pr, xs, xr, ys, yr, hs, hr,
):
    rows, det = pv.shape
    bpv = (bp0, bp1, bp2, bp3)
    n_proj, n_slab = lax.axis_size("proj"), lax.axis_size("slab")
    p, s = lax.axis_index("proj"), lax.axis_index("slab")
    x, c = p // 2, p % 2

    def at_p(d):
        return lax.rem(p + d + n_proj, n_proj)

    def at_s(d):
        return lax.rem(s + d + n_slab, n_slab)

    load_p = pltpu.make_async_copy(proj_ref, pv, lsem.at[0])
    load_k = pltpu.make_async_copy(strip_ref, ks, lsem.at[1])

    def load_b(jj):
        cols = pl.ds(pl.multiple_of(lax.rem(x + TURN[jj], 4) * WID, WID), WID)
        return pltpu.make_async_copy(bp_ref.at[:, :, cols], bpv[jj], lsem.at[3 + jj])

    load_k.start()
    load_p.start()

    barrier = pltpu.get_barrier_semaphore()
    greet = [(at_p(d), s) for d in (2, 4, 6)]
    greet += [(at_p(d), at_s(e)) for d in (-1, 1) for e in (-1, 0, 1)]
    greet += [(p, at_s(d)) for d in range(1, 16)]
    for dev in greet:
        pl.semaphore_signal(barrier, inc=1, device_id=dev, device_id_type=MESH)

    planv[...] = route(inter_ref[...], tiles_ref[...])
    to_smem = pltpu.make_async_copy(planv, plan, lsem.at[2])
    to_smem.start()
    rv[SLOTS] = jnp.zeros((64, WID), F32)
    for t in range(4):
        for b in range(det // WID):
            gainv[b, t] = jnp.broadcast_to(gain_ref[t : t + 1, b * WID : (b + 1) * WID], (8, WID))
    wlift[...] = lift_matrix(lift_ref[...], bias_ref[...])
    wmix[...] = mix_matrix(mix_ref[...])
    to_smem.wait()
    load_k.wait()
    load_p.wait()
    for jj in range(4):
        load_b(jj).start()

    def filt(b, dst):
        k = ks[pl.ds(pl.multiple_of((det - WID) - b * WID, WID), det), :]
        dst[...] = mm(pv[...], k).reshape(dst.shape)

    def weigh(b, src):
        cols = pl.ds(pl.multiple_of(b * WID, WID), WID)
        for q in range(SLOTS):
            f = src[plan[0, q]].reshape(8, 8, WID)
            g = gainv[b, plan[1, q // 4]]
            wv[q * 64 : q * 64 + 64, cols] = (f * g[None]).reshape(64, WID).astype(BF16)

    filt(0, fa)

    @pl.loop(0, det // WID // 2 - 1)
    def _(i):
        filt(2 * i + 1, fb)
        weigh(2 * i, fa)
        filt(2 * i + 2, fa)
        weigh(2 * i + 1, fb)

    filt(det // WID - 1, fb)
    weigh(det // WID - 2, fa)
    weigh(det // WID - 1, fb)

    pl.semaphore_wait(barrier, len(greet))

    def dots(jj, lo, hi):
        for b in range(lo, hi):
            out = mm(wv[b * WID : (b + 1) * WID, :], bpv[jj][plan[1, b]])
            rv[4 * b : 4 * b + 4] = out.reshape(4, 64, WID)

    def pair(jj):
        return pltpu.make_async_remote_copy(
            src_ref=psend.at[jj], dst_ref=prec.at[jj], send_sem=ps.at[jj], recv_sem=pr.at[jj],
            device_id=(p + 1 - 2 * c, s), device_id_type=MESH,
        )

    def sums(jj):
        @pl.loop(0, n_slab)
        def _(e):
            at = pl.ds(pl.multiple_of(e * 64, 64), 64)
            total = rv[plan[4, e]] + rv[plan[5, e]] + rv[plan[6, e]] + rv[plan[7, e]]
            low, high = total[:, :128], total[:, 128:]
            own[at, :] = jnp.where(c == 0, low, high)
            psend[jj, at, :] = jnp.where(c == 0, high, low).astype(BF16)

        pair(jj).start()

    def to_chip(jj):
        return pltpu.make_async_remote_copy(
            src_ref=xsend.at[jj], dst_ref=xrec.at[jj], send_sem=xs.at[jj], recv_sem=xr.at[jj],
            device_id=(at_p(2 * TURN[jj]), s), device_id_type=MESH,
        )

    def pass_on(jj):
        pair(jj).wait_recv()
        xsend[jj] = (own[...] + prec[jj].astype(F32)).astype(BF16)
        to_chip(jj).start()

    for jj in range(4):
        load_b(jj).wait()
        dots(jj, 0, 4)
        if jj:
            pass_on(jj - 1)
        dots(jj, 4, NB)
        sums(jj)

    pair(3).wait_recv()
    for jj in range(3):
        to_chip(jj).wait_recv()

    def total_of(e):
        at = pl.ds(pl.multiple_of(e * 64, 64), 64)
        total = own[at, :] + prec[3, at, :].astype(F32)
        for jj in range(3):
            total = total + xrec[jj, at, :].astype(F32)
        return total

    def to_slab(d):
        return pltpu.make_async_remote_copy(
            src_ref=ysend.at[d - 1], dst_ref=yrec.at[d - 1], send_sem=ys.at[d - 1], recv_sem=yr.at[d - 1],
            device_id=(p, at_s(d)), device_id_type=MESH,
        )

    @pl.loop(1, n_slab)
    def _(d):
        ysend[d - 1] = total_of(at_s(d)).astype(BF16)
        to_slab(d).start()

    vol[...] = total_of(s)

    @pl.loop(1, n_slab)
    def _(d):
        to_slab(d).wait_recv()
        vol[...] += yrec[d - 1].astype(F32)

    hsend[...] = vol[...].astype(BF16)
    halos = []
    for dp in (-1, 0, 1):
        for ds in (-1, 0, 1):
            if dp == 0 and ds == 0:
                continue
            src = {-1: (0, 32), 0: (0, 64), 1: (32, 32)}[ds]
            dst = {-1: 96, 0: 32, 1: 0}[ds]
            k = len(halos)
            halos.append(
                pltpu.make_async_remote_copy(
                    src_ref=hsend.at[pl.ds(src[0], src[1]), :],
                    dst_ref=hrec.at[1 - dp, pl.ds(dst, src[1]), :],
                    send_sem=hs.at[k], recv_sem=hr.at[k],
                    device_id=(at_p(dp), at_s(ds)), device_id_type=MESH,
                )
            )
    for h in halos:
        h.start()
    hrec[1, 32:96, :] = hsend[...]
    for h in halos:
        h.wait_recv()

    row, lane = iota((128, 128), 0), iota((128, 128), 1)
    inside = ((row >= 32) | (s > 0)) & ((row < 96) | (s < n_slab - 1))
    left = jnp.where(p > 0, hrec[0].astype(F32), 0.0)
    right = jnp.where(p < n_proj - 1, hrec[2].astype(F32), 0.0)
    mid = jnp.where(inside, hrec[1].astype(F32), 0.0)
    edge = jnp.where(inside, jnp.where(lane < 64, right, left), 0.0)
    cells = jnp.concatenate([mid, edge], axis=1)
    shifted = [pltpu.roll(cells, 1, 1), cells, pltpu.roll(cells, 255, 1)]
    shifted = [a.astype(BF16) for a in shifted]
    ones = jnp.ones((16, WID), BF16)
    flane = iota((NY * CH, WID), 1)
    keep = ((flane != 255) | (p > 0)) & ((flane != 128) | (p < n_proj - 1))
    mixed = []
    for zo in range(VZ + 2):
        window = jnp.concatenate([a[16 * zo : 16 * zo + 48] for a in shifted] + [ones], axis=0)
        live = keep
        if zo == 0:
            live = live & (s > 0)
        if zo == VZ + 1:
            live = live & (s < n_slab - 1)
        features = jnp.where(live, jnp.maximum(mm(wlift[...], window), 0.0), 0.0).astype(BF16)
        mixed.append(mm(wmix[...], features))
    for z in range(VZ):
        taps = []
        for dx in range(3):
            at = 16 * dx
            taps.append(sum(mixed[z + dz][48 * dz + at : 48 * dz + at + 16] for dz in range(3)))
        image = taps[1] + pltpu.roll(taps[0], 1, 1) + pltpu.roll(taps[2], 255, 1)
        out_ref[16 * z : 16 * z + 16, :] = vol[16 * z : 16 * z + 16, :] + image[:, :128]

    for jj in range(4):
        pair(jj).wait_send()
    for jj in range(3):
        to_chip(jj).wait_send()

    @pl.loop(1, n_slab)
    def _(d):
        to_slab(d).wait_send()

    for h in halos:
        h.wait_send()


def shards(
    projections, intersection, tiles, tile_gain, bp_matrix, lift_kernel, lift_bias, mix_kernel
):
    nblk, drows, det = projections.shape
    rows = nblk * drows
    hbm = pl.BlockSpec(memory_space=pl.ANY)
    vmem = pl.BlockSpec(memory_space=pltpu.VMEM)
    dma = pltpu.SemaphoreType.DMA
    image = pl.pallas_call(
        kernel,
        out_shape=jax.ShapeDtypeStruct((drows, 128), F32),
        in_specs=[hbm, hbm, vmem, vmem, vmem, hbm, vmem, vmem, vmem],
        out_specs=vmem,
        scratch_shapes=[
            pltpu.VMEM((rows, det), BF16),
            pltpu.VMEM((2 * det - WID, WID), BF16),
            pltpu.VMEM((4, det, WID), BF16),
            pltpu.VMEM((4, det, WID), BF16),
            pltpu.VMEM((4, det, WID), BF16),
            pltpu.VMEM((4, det, WID), BF16),
            pltpu.VMEM((nblk, drows, WID), F32),
            pltpu.VMEM((nblk, drows, WID), F32),
            pltpu.VMEM((det // WID, 4, 8, WID), F32),
            pltpu.VMEM((SLOTS * drows, det), BF16),
            pltpu.VMEM((SLOTS + 1, drows, WID), F32),
            pltpu.VMEM((rows, 128), F32),
            pltpu.VMEM((4, rows, 128), BF16),
            pltpu.VMEM((4, rows, 128), BF16),
            pltpu.VMEM((3, rows, 128), BF16),
            pltpu.VMEM((3, rows, 128), BF16),
            pltpu.VMEM((15, drows, 128), BF16),
            pltpu.VMEM((15, drows, 128), BF16),
            pltpu.VMEM((drows, 128), F32),
            pltpu.VMEM((drows, 128), BF16),
            pltpu.VMEM((3, 128, 128), BF16),
            pltpu.VMEM((NY * CH, 160), BF16),
            pltpu.VMEM((144, NY * CH), BF16),
            pltpu.VMEM((8, 128), jnp.int32),
            pltpu.SMEM((8, 128), jnp.int32),
            dma((7,)), dma((4,)), dma((4,)), dma((3,)), dma((3,)), dma((15,)), dma((15,)), dma((8,)), dma((8,)),
        ],
        compiler_params=pltpu.CompilerParams(
            vmem_limit_bytes=60 * 1024 * 1024, collective_id=0, has_side_effects=True
        ),
    )(
        projections.reshape(rows, det), jnp.asarray(lag_strip(det)), tile_gain, intersection.T, tiles.T,
        bp_matrix, lift_kernel, lift_bias.reshape(1, -1), mix_kernel,
    )
    return image.reshape(VZ, NY, 128)


def solution(mesh):
    split = ("proj", "slab")
    placed = (P(split, None, None), P(split, None), P(split, None), P(), P(), P(), P(), P())
    return jax.shard_map(
        shards, mesh=mesh, in_specs=placed, out_specs=P("slab", None, "proj"), check_vma=False
    )
```

time: 227 us -> 56.9 us (0.25)
  the two profiles are of different devices: /device:TPU:29 before, /device:TPU:1 now
where the time goes in v2:
time: 56.9 us; the launch traced here: 56.6 us
  Pallas kernels  55.2 us (97%)
  local copies, waits for them, and re-layouts  1.38 us (2%)
    pallas_call x1, Pallas kernels, shards(): pl.pallas_call(kernel, out_shape=jax.ShapeDtypeStruct((drows, 128), F32),...  55.2 us
    unnamed x1, local copies, waits for them, and re-layouts  1.38 us

profile of v2, /device:TPU:1, one launch (start us, length us, event | category | flops | bytes accessed | tf_op | source)
XLA Modules:
  0.0 56.6 jit_solution(18110876634050907139)
XLA Ops:
  0.0 55.2 %shard_map.91 = f32[64,128]{1,0:T(8,128)} custom-call(bf16[1024,2048]{1,0:T(8,128)(2,1)} %bitcast.5, bf16[3840,256]{1,0:T(8,128)(2,1)} %constant.2.clone.strip_ref, f32[4,2048]{1,0:T(4,128)} %gain_ref.1, s32[2,16]{1,0:T(2,128)} %bitcast.7, s32[2,16]{1,0:T(2,128)} %bitcast.8, bf16[4,2048,1024]{2,1,0:T(8,128)(2,1)} %bp_ref.1, f32[32,27]{1,0:T(8,128)} %lift_ref.1, ...), custom_call_target="tpu_custom_call" | custom-call | tf_op jit(solution)/shard_map/pallas_call | solution.py:336
  55.3 1.4 %copy.11 = f32[4,16,128]{2,1,0:T(8,128)} copy(f32[4,16,128]{2,1,0:T(8,128)} %bitcast.6) | data formatting | bytes 65536

commit v3 on v2

--- a/solution.py
+++ b/solution.py
@@ -79,23 +79,28 @@
 
 
 def lift_matrix(lift, bias):
-    rows, cols = NY * CH, 160
+    rows, cols = NY * CH, 448
     spread = hot((iota((rows, CH), 0) & (CH - 1)) == iota((rows, CH), 1))
-    taps = mm(spread, lift.astype(BF16)).astype(BF16)
+    head = lift.astype(BF16)
+    rest = (lift - head.astype(F32)).astype(BF16)
+    taps = mm(spread, head).astype(BF16)
+    fine = mm(spread, rest).astype(BF16)
     o, m = iota((27, cols), 0), iota((27, cols), 1)
-    dx, dz = m // 48, (m // 16) % 3
+    part = m // 144
+    dx, dz = (m % 144) // 48, (m // 16) % 3
     step = (iota((rows, cols), 1) & (NY - 1)) - iota((rows, cols), 0) // CH + 1
     out = jnp.zeros((rows, cols), F32)
     for dy in range(3):
-        pick = hot((o == 9 * dz + 3 * dy + dx) & (m < 144))
-        out = out + jnp.where(step == dy, mm(taps, pick), 0.0)
+        tap = o == 9 * dz + 3 * dy + dx
+        term = mm(taps, hot(tap & (part < 2))) + mm(fine, hot(tap & (part == 2)))
+        out = out + jnp.where(step == dy, term, 0.0)
     eye = iota((CH, CH), 0) == iota((CH, CH), 1)
     left = jnp.sum(jnp.where(eye, bias, 0.0), axis=1, keepdims=True)
     lane = iota((CH, cols), 1)
     table = jnp.zeros((CH, cols), F32)
     for k in range(3):
         head = left.astype(BF16).astype(F32)
-        table = table + jnp.where(lane == 144 + k, head, 0.0)
+        table = table + jnp.where(lane == 432 + k, head, 0.0)
         left = left - head
     return (out + mm(spread, table.astype(BF16))).astype(BF16)
 
@@ -116,7 +121,7 @@
 
 def kernel(
     proj_ref, strip_ref, gain_ref, inter_ref, tiles_ref, bp_ref, lift_ref, bias_ref, mix_ref, out_ref,
-    pv, ks, bp0, bp1, bp2, bp3, fa, fb, gainv, wv, rv, own, psend, prec, xsend, xrec, ysend, yrec, vol, hsend, hrec, wlift, wmix,
+    pv, ks, bp0, bp1, bp2, bp3, fa, fb, gainv, wv, rv, own, psend, prec, xsend, xrec, ysend, yrec, mine, vol, hrec, wlift, wmix,
     planv, plan, lsem, ps, pr, xs, xr, ys, yr, hs, hr,
 ):
     rows, det = pv.shape
@@ -131,15 +136,25 @@
     def at_s(d):
         return lax.rem(s + d + n_slab, n_slab)
 
-    load_p = pltpu.make_async_copy(proj_ref, pv, lsem.at[0])
-    load_k = pltpu.make_async_copy(strip_ref, ks, lsem.at[1])
+    quarter = rows // 4
+
+    def load_p(m):
+        part = pl.ds(m * quarter, quarter)
+        return pltpu.make_async_copy(proj_ref.at[part, :], pv.at[part, :], lsem.at[7 + m])
+
+    near, far = pl.ds(det - WID, det), pl.ds(0, det - WID)
+    load_near = pltpu.make_async_copy(strip_ref.at[near, :], ks.at[near, :], lsem.at[0])
+    load_far = pltpu.make_async_copy(strip_ref.at[far, :], ks.at[far, :], lsem.at[1])
+    load_near.start()
+    load_p(0).start()
+    load_far.start()
+    for m in range(1, 4):
+        load_p(m).start()
 
     def load_b(jj):
         cols = pl.ds(pl.multiple_of(lax.rem(x + TURN[jj], 4) * WID, WID), WID)
         return pltpu.make_async_copy(bp_ref.at[:, :, cols], bpv[jj], lsem.at[3 + jj])
 
-    load_k.start()
-    load_p.start()
 
     barrier = pltpu.get_barrier_semaphore()
     greet = [(at_p(d), s) for d in (2, 4, 6)]
@@ -158,10 +173,7 @@
     wlift[...] = lift_matrix(lift_ref[...], bias_ref[...])
     wmix[...] = mix_matrix(mix_ref[...])
     to_smem.wait()
-    load_k.wait()
-    load_p.wait()
-    for jj in range(4):
-        load_b(jj).start()
+    load_near.wait()
 
     def filt(b, dst):
         k = ks[pl.ds(pl.multiple_of((det - WID) - b * WID, WID), det), :]
@@ -174,7 +186,14 @@
             g = gainv[b, plan[1, q // 4]]
             wv[q * 64 : q * 64 + 64, cols] = (f * g[None]).reshape(64, WID).astype(BF16)
 
-    filt(0, fa)
+    near_block = ks[det - WID :, :]
+    for m in range(4):
+        load_p(m).wait()
+        if m == 3:
+            load_far.wait()
+            for jj in range(4):
+                load_b(jj).start()
+        fa[4 * m : 4 * m + 4] = mm(pv[m * quarter : (m + 1) * quarter, :], near_block).reshape(4, 64, WID)
 
     @pl.loop(0, det // WID // 2 - 1)
     def _(i):
@@ -211,55 +230,65 @@
 
         pair(jj).start()
 
+    def to_slab(jj, d):
+        k = jj * (n_slab - 1) + d - 1
+        return pltpu.make_async_remote_copy(
+            src_ref=ysend.at[k], dst_ref=yrec.at[k], send_sem=ys.at[k], recv_sem=yr.at[k],
+            device_id=(p, at_s(d)), device_id_type=MESH,
+        )
+
     def to_chip(jj):
         return pltpu.make_async_remote_copy(
             src_ref=xsend.at[jj], dst_ref=xrec.at[jj], send_sem=xs.at[jj], recv_sem=xr.at[jj],
             device_id=(at_p(2 * TURN[jj]), s), device_id_type=MESH,
         )
 
+    def spread(jj):
+        pair(jj).wait_recv()
+
+        def of(e):
+            at = pl.ds(pl.multiple_of(e * 64, 64), 64)
+            return own[at, :] + prec[jj, at, :].astype(F32)
+
+        @pl.loop(1, n_slab)
+        def _(d):
+            ysend[jj * (n_slab - 1) + d - 1] = of(at_s(d)).astype(BF16)
+            to_slab(jj, d).start()
+
+        mine[jj] = of(s)
+
+    def gather(jj):
+        @pl.loop(1, n_slab)
+        def _(d):
+            to_slab(jj, d).wait_recv()
+
+        total = mine[jj]
+        for d in range(n_slab - 1):
+            total = total + yrec[jj * (n_slab - 1) + d].astype(F32)
+        return total
+
     def pass_on(jj):
-        pair(jj).wait_recv()
-        xsend[jj] = (own[...] + prec[jj].astype(F32)).astype(BF16)
+        xsend[jj] = gather(jj)
         to_chip(jj).start()
 
     for jj in range(4):
         load_b(jj).wait()
         dots(jj, 0, 4)
         if jj:
-            pass_on(jj - 1)
+            spread(jj - 1)
         dots(jj, 4, NB)
+        if jj > 1:
+            pass_on(jj - 2)
         sums(jj)
 
-    pair(3).wait_recv()
+    pass_on(2)
+    spread(3)
+    total = gather(3)
     for jj in range(3):
         to_chip(jj).wait_recv()
-
-    def total_of(e):
-        at = pl.ds(pl.multiple_of(e * 64, 64), 64)
-        total = own[at, :] + prec[3, at, :].astype(F32)
-        for jj in range(3):
-            total = total + xrec[jj, at, :].astype(F32)
-        return total
-
-    def to_slab(d):
-        return pltpu.make_async_remote_copy(
-            src_ref=ysend.at[d - 1], dst_ref=yrec.at[d - 1], send_sem=ys.at[d - 1], recv_sem=yr.at[d - 1],
-            device_id=(p, at_s(d)), device_id_type=MESH,
-        )
-
-    @pl.loop(1, n_slab)
-    def _(d):
-        ysend[d - 1] = total_of(at_s(d)).astype(BF16)
-        to_slab(d).start()
-
-    vol[...] = total_of(s)
-
-    @pl.loop(1, n_slab)
-    def _(d):
-        to_slab(d).wait_recv()
-        vol[...] += yrec[d - 1].astype(F32)
-
-    hsend[...] = vol[...].astype(BF16)
+        total = total + xrec[jj]
+    vol[...] = total
+
     halos = []
     for dp in (-1, 0, 1):
         for ds in (-1, 0, 1):
@@ -270,7 +299,7 @@
             k = len(halos)
             halos.append(
                 pltpu.make_async_remote_copy(
-                    src_ref=hsend.at[pl.ds(src[0], src[1]), :],
+                    src_ref=vol.at[pl.ds(src[0], src[1]), :],
                     dst_ref=hrec.at[1 - dp, pl.ds(dst, src[1]), :],
                     send_sem=hs.at[k], recv_sem=hr.at[k],
                     device_id=(at_p(dp), at_s(ds)), device_id_type=MESH,
@@ -278,25 +307,26 @@
             )
     for h in halos:
         h.start()
-    hrec[1, 32:96, :] = hsend[...]
+    hrec[1, 32:96, :] = total
     for h in halos:
         h.wait_recv()
 
     row, lane = iota((128, 128), 0), iota((128, 128), 1)
     inside = ((row >= 32) | (s > 0)) & ((row < 96) | (s < n_slab - 1))
-    left = jnp.where(p > 0, hrec[0].astype(F32), 0.0)
-    right = jnp.where(p < n_proj - 1, hrec[2].astype(F32), 0.0)
-    mid = jnp.where(inside, hrec[1].astype(F32), 0.0)
+    left = jnp.where(p > 0, hrec[0], 0.0)
+    right = jnp.where(p < n_proj - 1, hrec[2], 0.0)
+    mid = jnp.where(inside, hrec[1], 0.0)
     edge = jnp.where(inside, jnp.where(lane < 64, right, left), 0.0)
     cells = jnp.concatenate([mid, edge], axis=1)
     shifted = [pltpu.roll(cells, 1, 1), cells, pltpu.roll(cells, 255, 1)]
-    shifted = [a.astype(BF16) for a in shifted]
+    high = [a.astype(BF16) for a in shifted]
+    low = [(a - h.astype(F32)).astype(BF16) for a, h in zip(shifted, high)]
     ones = jnp.ones((16, WID), BF16)
     flane = iota((NY * CH, WID), 1)
     keep = ((flane != 255) | (p > 0)) & ((flane != 128) | (p < n_proj - 1))
     mixed = []
     for zo in range(VZ + 2):
-        window = jnp.concatenate([a[16 * zo : 16 * zo + 48] for a in shifted] + [ones], axis=0)
+        window = jnp.concatenate([a[16 * zo : 16 * zo + 48] for a in high + low + high] + [ones], axis=0)
         live = keep
         if zo == 0:
             live = live & (s > 0)
@@ -317,9 +347,10 @@
     for jj in range(3):
         to_chip(jj).wait_send()
 
-    @pl.loop(1, n_slab)
-    def _(d):
-        to_slab(d).wait_send()
+    for jj in range(4):
+        @pl.loop(1, n_slab)
+        def _(d):
+            to_slab(jj, d).wait_send()
 
     for h in halos:
         h.wait_send()
@@ -353,18 +384,18 @@
             pltpu.VMEM((rows, 128), F32),
             pltpu.VMEM((4, rows, 128), BF16),
             pltpu.VMEM((4, rows, 128), BF16),
-            pltpu.VMEM((3, rows, 128), BF16),
-            pltpu.VMEM((3, rows, 128), BF16),
-            pltpu.VMEM((15, drows, 128), BF16),
-            pltpu.VMEM((15, drows, 128), BF16),
+            pltpu.VMEM((3, drows, 128), F32),
+            pltpu.VMEM((3, drows, 128), F32),
+            pltpu.VMEM((60, drows, 128), BF16),
+            pltpu.VMEM((60, drows, 128), BF16),
+            pltpu.VMEM((4, drows, 128), F32),
             pltpu.VMEM((drows, 128), F32),
-            pltpu.VMEM((drows, 128), BF16),
-            pltpu.VMEM((3, 128, 128), BF16),
-            pltpu.VMEM((NY * CH, 160), BF16),
+            pltpu.VMEM((3, 128, 128), F32),
+            pltpu.VMEM((NY * CH, 448), BF16),
             pltpu.VMEM((144, NY * CH), BF16),
             pltpu.VMEM((8, 128), jnp.int32),
             pltpu.SMEM((8, 128), jnp.int32),
-            dma((7,)), dma((4,)), dma((4,)), dma((3,)), dma((3,)), dma((15,)), dma((15,)), dma((8,)), dma((8,)),
+            dma((11,)), dma((4,)), dma((4,)), dma((3,)), dma((3,)), dma((60,)), dma((60,)), dma((8,)), dma((8,)),
         ],
         compiler_params=pltpu.CompilerParams(
             vmem_limit_bytes=60 * 1024 * 1024, collective_id=0, has_side_effects=True

time: 56.9 us -> 59.4 us (1.044)
  Pallas kernels: 55.2 us -> 57.7 us
    pallas_call x1, Pallas kernels: 55.2 us -> 57.7 us  [shards(): pl.pallas_call(kernel, out_shape=jax.ShapeDtypeStruct((drows, 128), F32),...]
where the time goes in v3:
time: 59.4 us; the launch traced here: 59.1 us
  Pallas kernels  57.7 us (97%)
  local copies, waits for them, and re-layouts  1.38 us (2%)
    pallas_call x1, Pallas kernels, shards(): pl.pallas_call(kernel, out_shape=jax.ShapeDtypeStruct((drows, 128), F32),...  57.7 us
    unnamed x1, local copies, waits for them, and re-layouts  1.38 us

profile of v3, /device:TPU:1, one launch (start us, length us, event | category | flops | bytes accessed | tf_op | source)
XLA Modules:
  0.0 59.1 jit_solution(14667951138169292617)
XLA Ops:
  0.0 57.7 %shard_map.91 = f32[64,128]{1,0:T(8,128)} custom-call(bf16[1024,2048]{1,0:T(8,128)(2,1)} %bitcast.5, bf16[3840,256]{1,0:T(8,128)(2,1)} %constant.2.clone.strip_ref, f32[4,2048]{1,0:T(4,128)} %gain_ref.1, s32[2,16]{1,0:T(2,128)} %bitcast.7, s32[2,16]{1,0:T(2,128)} %bitcast.8, bf16[4,2048,1024]{2,1,0:T(8,128)(2,1)} %bp_ref.1, f32[32,27]{1,0:T(8,128)} %lift_ref.1, ...), custom_call_target="tpu_custom_call" | custom-call | tf_op jit(solution)/shard_map/pallas_call | solution.py:367
  57.8 1.4 %copy.11 = f32[4,16,128]{2,1,0:T(8,128)} copy(f32[4,16,128]{2,1,0:T(8,128)} %bitcast.6) | data formatting | bytes 65536

commit v4 on v3

--- a/solution.py
+++ b/solution.py
@@ -15,8 +15,9 @@
 VZ = 4
 NY = 16
 CH = 32
-NB = 11
-SLOTS = 4 * NB
+GRP = 3
+NB = 13
+SLOTS = GRP * NB
 WID = 256
 TURN = (2, 1, 3, 0)
 
@@ -56,10 +57,10 @@
     total = jnp.zeros((1, 128), jnp.int32)
     for t in range(3):
         count = jnp.sum(jnp.where(tb == t, 1, 0), axis=0, keepdims=True)
-        total = total + ((count + 3) >> 2)
+        total = total + (((count + GRP - 1) * 171) >> 9)
         ends.append(total)
     base = jnp.where(tb == 0, 0, jnp.where(tb == 1, ends[0], jnp.where(tb == 2, ends[1], ends[2])))
-    slot = 4 * base + rank(tb)
+    slot = GRP * base + rank(tb)
     view_row = jnp.sum(jnp.where(slot == lane, row & (nv - 1), 0), axis=0, keepdims=True)
     tile_row = sum(jnp.where(lane1 >= e, 1, 0) for e in ends)
     order = rank(sb)
@@ -121,7 +122,7 @@
 
 def kernel(
     proj_ref, strip_ref, gain_ref, inter_ref, tiles_ref, bp_ref, lift_ref, bias_ref, mix_ref, out_ref,
-    pv, ks, bp0, bp1, bp2, bp3, fa, fb, gainv, wv, rv, own, psend, prec, xsend, xrec, ysend, yrec, mine, vol, hrec, wlift, wmix,
+    pv, ks, bp0, bp1, bp2, bp3, fa, fb, gainv, wv, rv, own, psend, prec, xsend, xrec, ysend, yrec, bsend, brec, mine, vol, hsend, hrec, wlift, wmix,
     planv, plan, lsem, ps, pr, xs, xr, ys, yr, hs, hr,
 ):
     rows, det = pv.shape
@@ -183,7 +184,7 @@
         cols = pl.ds(pl.multiple_of(b * WID, WID), WID)
         for q in range(SLOTS):
             f = src[plan[0, q]].reshape(8, 8, WID)
-            g = gainv[b, plan[1, q // 4]]
+            g = gainv[b, plan[1, q // GRP]]
             wv[q * 64 : q * 64 + 64, cols] = (f * g[None]).reshape(64, WID).astype(BF16)
 
     near_block = ks[det - WID :, :]
@@ -210,8 +211,8 @@
 
     def dots(jj, lo, hi):
         for b in range(lo, hi):
-            out = mm(wv[b * WID : (b + 1) * WID, :], bpv[jj][plan[1, b]])
-            rv[4 * b : 4 * b + 4] = out.reshape(4, 64, WID)
+            out = mm(wv[b * GRP * 64 : (b + 1) * GRP * 64, :], bpv[jj][plan[1, b]])
+            rv[GRP * b : GRP * b + GRP] = out.reshape(GRP, 64, WID)
 
     def pair(jj):
         return pltpu.make_async_remote_copy(
@@ -230,64 +231,70 @@
 
         pair(jj).start()
 
-    def to_slab(jj, d):
-        k = jj * (n_slab - 1) + d - 1
+    def to_slab(k, d):
+        k = k * (n_slab - 1) + d - 1
         return pltpu.make_async_remote_copy(
             src_ref=ysend.at[k], dst_ref=yrec.at[k], send_sem=ys.at[k], recv_sem=yr.at[k],
             device_id=(p, at_s(d)), device_id_type=MESH,
         )
 
     def to_chip(jj):
+        src, dst = (bsend, brec) if jj == 0 else (xsend.at[jj - 1], xrec.at[jj - 1])
         return pltpu.make_async_remote_copy(
-            src_ref=xsend.at[jj], dst_ref=xrec.at[jj], send_sem=xs.at[jj], recv_sem=xr.at[jj],
+            src_ref=src, dst_ref=dst, send_sem=xs.at[jj], recv_sem=xr.at[jj],
             device_id=(at_p(2 * TURN[jj]), s), device_id_type=MESH,
         )
 
-    def spread(jj):
+    def spread(k, jj):
         pair(jj).wait_recv()
+        if jj == 3:
+            to_chip(1).wait_recv()
+            to_chip(2).wait_recv()
 
         def of(e):
             at = pl.ds(pl.multiple_of(e * 64, 64), 64)
-            return own[at, :] + prec[jj, at, :].astype(F32)
-
-        @pl.loop(1, n_slab)
+            total = own[at, :] + prec[jj, at, :].astype(F32)
+            if jj == 3:
+                total = total + (xrec[0, at, :].astype(F32) + xrec[1, at, :].astype(F32))
+            return total
+
+        @pl.loop(1, n_slab, unroll=5)
         def _(d):
-            ysend[jj * (n_slab - 1) + d - 1] = of(at_s(d)).astype(BF16)
-            to_slab(jj, d).start()
-
-        mine[jj] = of(s)
-
-    def gather(jj):
-        @pl.loop(1, n_slab)
-        def _(d):
-            to_slab(jj, d).wait_recv()
-
-        total = mine[jj]
-        for d in range(n_slab - 1):
-            total = total + yrec[jj * (n_slab - 1) + d].astype(F32)
+            ysend[k * (n_slab - 1) + d - 1] = of(at_s(d)).astype(BF16)
+            to_slab(k, d).start()
+
+        mine[k] = of(s)
+
+    def gather(k):
+        total = mine[k]
+        for d in range(1, n_slab):
+            to_slab(k, d).wait_recv()
+            total = total + yrec[k * (n_slab - 1) + d - 1].astype(F32)
         return total
 
     def pass_on(jj):
-        xsend[jj] = gather(jj)
+        pair(jj).wait_recv()
+        xsend[jj - 1] = (own[...] + prec[jj].astype(F32)).astype(BF16)
         to_chip(jj).start()
 
     for jj in range(4):
         load_b(jj).wait()
-        dots(jj, 0, 4)
-        if jj:
-            spread(jj - 1)
-        dots(jj, 4, NB)
-        if jj > 1:
-            pass_on(jj - 2)
+        dots(jj, 0, 5)
+        if jj == 1:
+            spread(0, 0)
+        elif jj > 1:
+            pass_on(jj - 1)
+        dots(jj, 5, NB)
+        if jj == 2:
+            bsend[...] = gather(0)
+            to_chip(0).start()
         sums(jj)
 
-    pass_on(2)
-    spread(3)
-    total = gather(3)
-    for jj in range(3):
-        to_chip(jj).wait_recv()
-        total = total + xrec[jj]
+    spread(1, 3)
+    to_chip(0).wait_recv()
+    total = gather(1) + brec[...]
     vol[...] = total
+    hsend[...] = total.astype(BF16)
 
     halos = []
     for dp in (-1, 0, 1):
@@ -299,7 +306,7 @@
             k = len(halos)
             halos.append(
                 pltpu.make_async_remote_copy(
-                    src_ref=vol.at[pl.ds(src[0], src[1]), :],
+                    src_ref=hsend.at[pl.ds(src[0], src[1]), :],
                     dst_ref=hrec.at[1 - dp, pl.ds(dst, src[1]), :],
                     send_sem=hs.at[k], recv_sem=hr.at[k],
                     device_id=(at_p(dp), at_s(ds)), device_id_type=MESH,
@@ -307,15 +314,15 @@
             )
     for h in halos:
         h.start()
-    hrec[1, 32:96, :] = total
     for h in halos:
         h.wait_recv()
 
     row, lane = iota((128, 128), 0), iota((128, 128), 1)
     inside = ((row >= 32) | (s > 0)) & ((row < 96) | (s < n_slab - 1))
-    left = jnp.where(p > 0, hrec[0], 0.0)
-    right = jnp.where(p < n_proj - 1, hrec[2], 0.0)
-    mid = jnp.where(inside, hrec[1], 0.0)
+    left = jnp.where(p > 0, hrec[0].astype(F32), 0.0)
+    right = jnp.where(p < n_proj - 1, hrec[2].astype(F32), 0.0)
+    mid = jnp.concatenate([hrec[1, :32].astype(F32), total, hrec[1, 96:].astype(F32)], axis=0)
+    mid = jnp.where(inside, mid, 0.0)
     edge = jnp.where(inside, jnp.where(lane < 64, right, left), 0.0)
     cells = jnp.concatenate([mid, edge], axis=1)
     shifted = [pltpu.roll(cells, 1, 1), cells, pltpu.roll(cells, 255, 1)]
@@ -347,10 +354,10 @@
     for jj in range(3):
         to_chip(jj).wait_send()
 
-    for jj in range(4):
+    for k in range(2):
         @pl.loop(1, n_slab)
         def _(d):
-            to_slab(jj, d).wait_send()
+            to_slab(k, d).wait_send()
 
     for h in halos:
         h.wait_send()
@@ -384,18 +391,21 @@
             pltpu.VMEM((rows, 128), F32),
             pltpu.VMEM((4, rows, 128), BF16),
             pltpu.VMEM((4, rows, 128), BF16),
-            pltpu.VMEM((3, drows, 128), F32),
-            pltpu.VMEM((3, drows, 128), F32),
-            pltpu.VMEM((60, drows, 128), BF16),
-            pltpu.VMEM((60, drows, 128), BF16),
-            pltpu.VMEM((4, drows, 128), F32),
+            pltpu.VMEM((2, rows, 128), BF16),
+            pltpu.VMEM((2, rows, 128), BF16),
+            pltpu.VMEM((30, drows, 128), BF16),
+            pltpu.VMEM((30, drows, 128), BF16),
             pltpu.VMEM((drows, 128), F32),
-            pltpu.VMEM((3, 128, 128), F32),
+            pltpu.VMEM((drows, 128), F32),
+            pltpu.VMEM((2, drows, 128), F32),
+            pltpu.VMEM((drows, 128), F32),
+            pltpu.VMEM((drows, 128), BF16),
+            pltpu.VMEM((3, 128, 128), BF16),
             pltpu.VMEM((NY * CH, 448), BF16),
             pltpu.VMEM((144, NY * CH), BF16),
             pltpu.VMEM((8, 128), jnp.int32),
             pltpu.SMEM((8, 128), jnp.int32),
-            dma((11,)), dma((4,)), dma((4,)), dma((3,)), dma((3,)), dma((60,)), dma((60,)), dma((8,)), dma((8,)),
+            dma((11,)), dma((4,)), dma((4,)), dma((3,)), dma((3,)), dma((30,)), dma((30,)), dma((8,)), dma((8,)),
         ],
         compiler_params=pltpu.CompilerParams(
             vmem_limit_bytes=60 * 1024 * 1024, collective_id=0, has_side_effects=True

time: 59.4 us -> 59.6 us (level)
  no operation moved by 1% of the time
where the time goes in v4:
time: 59.6 us; the launch traced here: 59.4 us
  Pallas kernels  58 us (97%)
  local copies, waits for them, and re-layouts  1.38 us (2%)
    pallas_call x1, Pallas kernels, shards(): pl.pallas_call(kernel, out_shape=jax.ShapeDtypeStruct((drows, 128), F32),...  58 us
    unnamed x1, local copies, waits for them, and re-layouts  1.38 us

profile of v4, /device:TPU:1, one launch (start us, length us, event | category | flops | bytes accessed | tf_op | source)
XLA Modules:
  0.0 59.4 jit_solution(13385307710268700134)
XLA Ops:
  0.0 58.0 %shard_map.91 = f32[64,128]{1,0:T(8,128)} custom-call(bf16[1024,2048]{1,0:T(8,128)(2,1)} %bitcast.5, bf16[3840,256]{1,0:T(8,128)(2,1)} %constant.2.clone.strip_ref, f32[4,2048]{1,0:T(4,128)} %gain_ref.1, s32[2,16]{1,0:T(2,128)} %bitcast.7, s32[2,16]{1,0:T(2,128)} %bitcast.8, bf16[4,2048,1024]{2,1,0:T(8,128)(2,1)} %bp_ref.1, f32[32,27]{1,0:T(8,128)} %lift_ref.1, ...), custom_call_target="tpu_custom_call" | custom-call | tf_op jit(solution)/shard_map/pallas_call | solution.py:374
  58.0 1.4 %copy.11 = f32[4,16,128]{2,1,0:T(8,128)} copy(f32[4,16,128]{2,1,0:T(8,128)} %bitcast.6) | data formatting | bytes 65536

commit v5 on v2

--- a/solution.py
+++ b/solution.py
@@ -15,8 +15,9 @@
 VZ = 4
 NY = 16
 CH = 32
-NB = 11
-SLOTS = 4 * NB
+GRP = 3
+NB = 13
+SLOTS = GRP * NB
 WID = 256
 TURN = (2, 1, 3, 0)
 
@@ -56,10 +57,10 @@
     total = jnp.zeros((1, 128), jnp.int32)
     for t in range(3):
         count = jnp.sum(jnp.where(tb == t, 1, 0), axis=0, keepdims=True)
-        total = total + ((count + 3) >> 2)
+        total = total + (((count + GRP - 1) * 171) >> 9)
         ends.append(total)
     base = jnp.where(tb == 0, 0, jnp.where(tb == 1, ends[0], jnp.where(tb == 2, ends[1], ends[2])))
-    slot = 4 * base + rank(tb)
+    slot = GRP * base + rank(tb)
     view_row = jnp.sum(jnp.where(slot == lane, row & (nv - 1), 0), axis=0, keepdims=True)
     tile_row = sum(jnp.where(lane1 >= e, 1, 0) for e in ends)
     order = rank(sb)
@@ -165,19 +166,18 @@
 
     def filt(b, dst):
         k = ks[pl.ds(pl.multiple_of((det - WID) - b * WID, WID), det), :]
-        dst[...] = mm(pv[...], k).reshape(dst.shape)
+        dst[...] = mm(pv[...], k).astype(BF16).astype(F32).reshape(dst.shape)
 
     def weigh(b, src):
         cols = pl.ds(pl.multiple_of(b * WID, WID), WID)
         for q in range(SLOTS):
             f = src[plan[0, q]].reshape(8, 8, WID)
-            g = gainv[b, plan[1, q // 4]]
+            g = gainv[b, plan[1, q // GRP]]
             wv[q * 64 : q * 64 + 64, cols] = (f * g[None]).reshape(64, WID).astype(BF16)
 
     filt(0, fa)
 
-    @pl.loop(0, det // WID // 2 - 1)
-    def _(i):
+    for i in range(det // WID // 2 - 1):
         filt(2 * i + 1, fb)
         weigh(2 * i, fa)
         filt(2 * i + 2, fa)
@@ -191,8 +191,8 @@
 
     def dots(jj, lo, hi):
         for b in range(lo, hi):
-            out = mm(wv[b * WID : (b + 1) * WID, :], bpv[jj][plan[1, b]])
-            rv[4 * b : 4 * b + 4] = out.reshape(4, 64, WID)
+            out = mm(wv[b * GRP * 64 : (b + 1) * GRP * 64, :], bpv[jj][plan[1, b]])
+            rv[GRP * b : GRP * b + GRP] = out.reshape(GRP, 64, WID)
 
     def pair(jj):
         return pltpu.make_async_remote_copy(
@@ -252,14 +252,12 @@
         ysend[d - 1] = total_of(at_s(d)).astype(BF16)
         to_slab(d).start()
 
-    vol[...] = total_of(s)
-
-    @pl.loop(1, n_slab)
-    def _(d):
+    total = total_of(s)
+    for d in range(1, n_slab):
         to_slab(d).wait_recv()
-        vol[...] += yrec[d - 1].astype(F32)
-
-    hsend[...] = vol[...].astype(BF16)
+        total = total + yrec[d - 1].astype(F32)
+    vol[...] = total
+    hsend[...] = total.astype(BF16)
     halos = []
     for dp in (-1, 0, 1):
         for ds in (-1, 0, 1):

time: 56.9 us -> 56 us (0.984)
  Pallas kernels: 55.2 us -> 54.3 us
    pallas_call x1, Pallas kernels: 55.2 us -> 54.3 us  [shards(): pl.pallas_call(kernel, out_shape=jax.ShapeDtypeStruct((drows, 128), F32),...]
where the time goes in v5:
time: 56 us; the launch traced here: 55.7 us
  Pallas kernels  54.3 us (97%)
  local copies, waits for them, and re-layouts  1.38 us (2%)
    pallas_call x1, Pallas kernels, shards(): pl.pallas_call(kernel, out_shape=jax.ShapeDtypeStruct((drows, 128), F32),...  54.3 us
    unnamed x1, local copies, waits for them, and re-layouts  1.38 us

profile of v5, /device:TPU:1, one launch (start us, length us, event | category | flops | bytes accessed | tf_op | source)
XLA Modules:
  0.0 55.7 jit_solution(16673937444049487730)
XLA Ops:
  0.0 54.3 %shard_map.91 = f32[64,128]{1,0:T(8,128)} custom-call(bf16[1024,2048]{1,0:T(8,128)(2,1)} %bitcast.5, bf16[3840,256]{1,0:T(8,128)(2,1)} %constant.2.clone.strip_ref, f32[4,2048]{1,0:T(4,128)} %gain_ref.1, s32[2,16]{1,0:T(2,128)} %bitcast.7, s32[2,16]{1,0:T(2,128)} %bitcast.8, bf16[4,2048,1024]{2,1,0:T(8,128)(2,1)} %bp_ref.1, f32[32,27]{1,0:T(8,128)} %lift_ref.1, ...), custom_call_target="tpu_custom_call" | custom-call | tf_op jit(solution)/shard_map/pallas_call | solution.py:334
  54.3 1.4 %copy.11 = f32[4,16,128]{2,1,0:T(8,128)} copy(f32[4,16,128]{2,1,0:T(8,128)} %bitcast.6) | data formatting | bytes 65536

commit v6 on v5

--- a/solution.py
+++ b/solution.py
@@ -224,10 +224,11 @@
 
     for jj in range(4):
         load_b(jj).wait()
-        dots(jj, 0, 4)
+        cut = 7 if jj < 3 else 4
+        dots(jj, 0, cut)
         if jj:
             pass_on(jj - 1)
-        dots(jj, 4, NB)
+        dots(jj, cut, NB)
         sums(jj)
 
     pair(3).wait_recv()

time: 56 us -> 55.4 us (0.989)
    pallas_call x1, Pallas kernels: 54.3 us -> 53.8 us  [shards(): pl.pallas_call(kernel, out_shape=jax.ShapeDtypeStruct((drows, 128), F32),...]
where the time goes in v6:
time: 55.4 us; the launch traced here: 55.1 us
  Pallas kernels  53.8 us (97%)
  local copies, waits for them, and re-layouts  1.38 us (2%)
    pallas_call x1, Pallas kernels, shards(): pl.pallas_call(kernel, out_shape=jax.ShapeDtypeStruct((drows, 128), F32),...  53.8 us
    unnamed x1, local copies, waits for them, and re-layouts  1.38 us

profile of v6, /device:TPU:1, one launch (start us, length us, event | category | flops | bytes accessed | tf_op | source)
XLA Modules:
  0.0 55.1 jit_solution(6265471929803041377)
XLA Ops:
  0.0 53.8 %shard_map.91 = f32[64,128]{1,0:T(8,128)} custom-call(bf16[1024,2048]{1,0:T(8,128)(2,1)} %bitcast.5, bf16[3840,256]{1,0:T(8,128)(2,1)} %constant.2.clone.strip_ref, f32[4,2048]{1,0:T(4,128)} %gain_ref.1, s32[2,16]{1,0:T(2,128)} %bitcast.7, s32[2,16]{1,0:T(2,128)} %bitcast.8, bf16[4,2048,1024]{2,1,0:T(8,128)(2,1)} %bp_ref.1, f32[32,27]{1,0:T(8,128)} %lift_ref.1, ...), custom_call_target="tpu_custom_call" | custom-call | tf_op jit(solution)/shard_map/pallas_call | solution.py:335
  53.8 1.4 %copy.11 = f32[4,16,128]{2,1,0:T(8,128)} copy(f32[4,16,128]{2,1,0:T(8,128)} %bitcast.6) | data formatting | bytes 65536
